TPU v7x, 512 devices: a whole 4x4x16 slice. The times are simulated.
512 devices in a mesh: ctx: 128 (over z, y, core), head: 4 (over x).
Axes of the slice: x: 4, y: 4, z: 16, core: 2. Of those that a mesh axis runs over, the one named last changes fastest.
Arguments:
- queries: bfloat16 [65536, 1024], P('ctx', 'head'), parts along dimension 1, may hold values from -100 to 100
- keys: bfloat16 [65536, 1024], P('ctx', 'head'), parts along dimension 1, may hold values from -5 to 5
- values: bfloat16 [65536, 1024], P('ctx', 'head'), parts along dimension 1, may hold values from -5 to 5
Outputs:
- attended: bfloat16 [65536, 1024], P('ctx', 'head'), parts along dimension 1
There are 4 independent parts, one for each index of `head`. A program takes and returns all parts, laid end to end along the dimension named above; each array names one. Nothing has to cross between parts.
All inputs are finite; a program needn't handle non-finite values.
Results may differ from a plain program's by a relative error of at most 0.001.
Values sent between devices are 32-bit elements; how exact they have to be, the bound alone decides.
A program may use at most 64 MiB of HBM per device.

v0:
```python
import jax
import jax.numpy as jnp
from jax import lax
from jax.sharding import PartitionSpec as P

NB = 128
HEADS = 2
DH = 128


def partner_2(value, axis, stride):
    mask = 2**stride
    pairs = [(source, source ^ mask) for source in range(lax.axis_size(axis))]
    return lax.ppermute(value, axis, pairs)


def coarsen(field, factor):
    rows = field.shape[0] // factor
    return jnp.mean(field.reshape(rows, factor, field.shape[1], field.shape[2]), axis=1)


def pair_terms(query_blocks, key_blocks, value_blocks, weight):
    scale = DH ** (-0.5)
    scores = (
        jnp.einsum("bihd,bjhd->bhij", query_blocks, key_blocks, precision=lax.Precision.HIGHEST)
        * scale
    )
    top = jnp.max(scores, axis=-1)
    probs = jnp.exp(scores - top[..., None])
    den = weight * jnp.sum(probs, axis=-1)
    num = weight * jnp.einsum(
        "bhij,bjhd->bihd", probs, value_blocks, precision=lax.Precision.HIGHEST
    )
    heads = query_blocks.shape[2]
    return (
        jnp.swapaxes(top, 1, 2).reshape(-1, heads),
        jnp.swapaxes(den, 1, 2).reshape(-1, heads),
        num.reshape(-1, heads, query_blocks.shape[3]),
    )


def sibling(field):
    supers = field.shape[0] // NB
    paired = field.reshape(supers // 2, 2, NB, field.shape[1], field.shape[2])[:, ::-1]
    return paired.reshape(supers, NB, field.shape[1], field.shape[2])


def expand(field, factor):
    wide = jnp.broadcast_to(field[:, None], (field.shape[0], factor) + field.shape[1:])
    return wide.reshape((field.shape[0] * factor,) + field.shape[1:])


def on_device(queries, keys, values):
    tokens_here = queries.shape[0]
    q_full = queries.astype(jnp.float32).reshape(tokens_here, HEADS, DH)
    k_full = keys.astype(jnp.float32).reshape(tokens_here, HEADS, DH)
    v_full = values.astype(jnp.float32).reshape(tokens_here, HEADS, DH)
    group = 2 * NB
    shape_near = (tokens_here // group, group, HEADS, DH)
    levels = [
        (
            1,
            pair_terms(
                q_full.reshape(shape_near),
                k_full.reshape(shape_near),
                v_full.reshape(shape_near),
                1.0,
            ),
        )
    ]
    base = (tokens_here // NB).bit_length() - 1
    factor = 2**1
    q_coarse = coarsen(q_full, factor)
    supers = q_coarse.shape[0] // NB
    levels.append(
        (
            factor,
            pair_terms(
                q_coarse.reshape(supers, NB, HEADS, DH),
                sibling(coarsen(k_full, factor)),
                sibling(coarsen(v_full, factor)),
                float(factor),
            ),
        )
    )
    position = lax.axis_index("ctx")
    depth = lax.axis_size("ctx").bit_length() - 1
    group_k = coarsen(k_full, 2**base)
    group_v = coarsen(v_full, 2**base)
    for bit in range(depth):
        factor = 2 ** (base + bit)
        q_coarse = coarsen(q_full, factor)
        other_k, other_v = partner_2((group_k, group_v), "ctx", bit)
        if bit + 1 < depth:
            upper_half = position // 2**bit % 2 == 1
            lower_k = jnp.where(upper_half, other_k, group_k)
            higher_k = jnp.where(upper_half, group_k, other_k)
            lower_v = jnp.where(upper_half, other_v, group_v)
            higher_v = jnp.where(upper_half, group_v, other_v)
            group_k = coarsen(jnp.concatenate([lower_k, higher_k], axis=0), 2)
            group_v = coarsen(jnp.concatenate([lower_v, higher_v], axis=0), 2)
        levels.append(
            (factor, pair_terms(q_coarse[None], other_k[None], other_v[None], float(factor)))
        )
    largest = None
    for factor, terms in levels:
        spread = expand(terms[0], factor)
        largest = spread if largest is None else jnp.maximum(largest, spread)
    numer = jnp.zeros((tokens_here, HEADS, DH), jnp.float32)
    denom = jnp.zeros((tokens_here, HEADS), jnp.float32)
    for factor, terms in levels:
        weight = jnp.exp(expand(terms[0], factor) - largest)
        denom = denom + weight * expand(terms[1], factor)
        numer = numer + weight[..., None] * expand(terms[2], factor)
    attended = numer / denom[..., None]
    return attended.reshape(tokens_here, HEADS * DH).astype(jnp.bfloat16)


def solution(mesh):
    in_specs = (P("ctx", "head"), P("ctx", "head"), P("ctx", "head"))
    out_specs = P("ctx", "head")
    return jax.shard_map(
        on_device, mesh=mesh, in_specs=in_specs, out_specs=out_specs, check_vma=False
    )
```

profile of v0, /device:TPU:6, one launch (start us, length us, event | category | flops | bytes accessed | tf_op | source)
XLA Modules:
  0.0 152.6 jit_solution(14657207856948749087)
XLA Ops:
  0.0 1.2 reshape_reshape.50
  2.3 1.9 %collective-permute-start = (f32[128,2,128]{2,0,1:T(8,128)}, f32[128,2,128]{2,0,1:T(8,128)}, u32[]{:S(2)}, u32[]{:S(2)}) collective-permute-start(f32[128,2,128]{2,0,1:T(8,128)} %copy_multiply_fusion.2), channel_id=1, source_target_pairs={{0,4},{4,0},{8,12},{12,8},{16,20},{20,16},{24,28},{28,24},{32,36},... | collective-permute-start | bytes 393224 | tf_op jit(solution)/shard_map/ppermute | solution.py:14
  5.6 2.4 %collective-permute-start.7 = (f32[128,2,128]{2,0,1:T(8,128)}, f32[128,2,128]{2,0,1:T(8,128)}, u32[]{:S(2)}, u32[]{:S(2)}) collective-permute-start(f32[128,2,128]{2,0,1:T(8,128)} %copy_multiply_fusion.1), channel_id=1, source_target_pairs={{0,4},{4,0},{8,12},{12,8},{16,20},{20,16},{24,28},{28,24},{32,36},... | collective-permute-start | bytes 393224 | tf_op jit(solution)/shard_map/ppermute | solution.py:14
  12.5 1.3 fusion
  15.2 1.1 convolution_bitcast_fusion
  17.7 1.0 copy.169
  18.7 0.9 copy.170
  20.4 1.7 %reshape.797 = f32[512,2]{0,1:T(2,128)} reshape(f32[256,2,2]{1,0,2:T(8,128)} %broadcast_in_dim.97) | data formatting | bytes 8192 | tf_op jit(solution)/shard_map/reshape | solution.py:50
  23.0 1.7 %reshape.826 = f32[512,2]{0,1:T(2,128)} reshape(f32[256,2,2]{1,0,2:T(8,128)} %broadcast_in_dim.129) | data formatting | bytes 8192 | tf_op jit(solution)/shard_map/reshape | solution.py:50
  24.7 1.1 reduce_sum.304
  27.7 0.9 broadcast_select_fusion.23
  29.0 3.5 %collective-permute-start.1 = (f32[128,2,128]{2,0,1:T(8,128)S(1)}, f32[128,2,128]{2,0,1:T(8,128)S(1)}, u32[]{:S(2)}, u32[]{:S(2)}) collective-permute-start(f32[128,2,128]{2,0,1:T(8,128)S(1)} %broadcast_multiply_fusion.11), channel_id=1, source_target_pairs={{0,8},{4,12},{8,0},{12,4},{16,24},{20,28},{24,16},{28,20},{32,40},... | collective-permute-start | bytes 393224 | tf_op jit(solution)/shard_map/ppermute | solution.py:14
  32.5 0.9 broadcast_select_fusion.21
  33.8 2.7 %collective-permute-start.8 = (f32[128,2,128]{2,0,1:T(8,128)S(1)}, f32[128,2,128]{2,0,1:T(8,128)S(1)}, u32[]{:S(2)}, u32[]{:S(2)}) collective-permute-start(f32[128,2,128]{2,0,1:T(8,128)S(1)} %broadcast_multiply_fusion.5), channel_id=1, source_target_pairs={{0,8},{4,12},{8,0},{12,4},{16,24},{20,28},{24,16},{28,20},{32,40},... | collective-permute-start | bytes 393224 | tf_op jit(solution)/shard_map/ppermute | solution.py:14
  36.5 1.3 fusion.65
  37.8 1.3 fusion.1
  41.1 5.1 %collective-permute-start.2 = (f32[128,2,128]{2,0,1:T(8,128)S(1)}, f32[128,2,128]{2,0,1:T(8,128)S(1)}, u32[]{:S(2)}, u32[]{:S(2)}) collective-permute-start(f32[128,2,128]{2,0,1:T(8,128)S(1)} %broadcast_multiply_fusion.10), channel_id=1, source_target_pairs={{0,16},{4,20},{8,24},{12,28},{16,0},{20,4},{24,8},{28,12},{32,48},... | collective-permute-start | bytes 393224 | tf_op jit(solution)/shard_map/ppermute | solution.py:14
  47.6 2.3 %collective-permute-start.9 = (f32[128,2,128]{2,0,1:T(8,128)S(1)}, f32[128,2,128]{2,0,1:T(8,128)S(1)}, u32[]{:S(2)}, u32[]{:S(2)}) collective-permute-start(f32[128,2,128]{2,0,1:T(8,128)S(1)} %broadcast_multiply_fusion.4), channel_id=1, source_target_pairs={{0,16},{4,20},{8,24},{12,28},{16,0},{20,4},{24,8},{28,12},{32,48},... | collective-permute-start | bytes 393224 | tf_op jit(solution)/shard_map/ppermute | solution.py:14
  50.3 3.8 %collective-permute-start.3 = (f32[128,2,128]{2,0,1:T(8,128)S(1)}, f32[128,2,128]{2,0,1:T(8,128)S(1)}, u32[]{:S(2)}, u32[]{:S(2)}) collective-permute-start(f32[128,2,128]{2,0,1:T(8,128)S(1)} %broadcast_multiply_fusion.9), channel_id=1, source_target_pairs={{0,32},{4,36},{8,40},{12,44},{16,48},{20,52},{24,56},{28,60},{32,0... | collective-permute-start | bytes 393224 | tf_op jit(solution)/shard_map/ppermute | solution.py:14
  54.1 1.9 %collective-permute-done.9 = f32[128,2,128]{2,0,1:T(8,128)S(1)} collective-permute-done((f32[128,2,128]{2,0,1:T(8,128)S(1)}, f32[128,2,128]{2,0,1:T(8,128)S(1)}, u32[]{:S(2)}, u32[]{:S(2)}) %collective-permute-start.9) | collective-permute-done | bytes 131104 | tf_op jit(solution)/shard_map/ppermute | solution.py:14
  56.4 3.8 %collective-permute-start.10 = (f32[128,2,128]{2,0,1:T(8,128)S(1)}, f32[128,2,128]{2,0,1:T(8,128)S(1)}, u32[]{:S(2)}, u32[]{:S(2)}) collective-permute-start(f32[128,2,128]{2,0,1:T(8,128)S(1)} %broadcast_multiply_fusion.3), channel_id=1, source_target_pairs={{0,32},{4,36},{8,40},{12,44},{16,48},{20,52},{24,56},{28,60},{32,0... | collective-permute-start | bytes 393224 | tf_op jit(solution)/shard_map/ppermute | solution.py:14
  62.4 5.2 %collective-permute-start.4 = (f32[128,2,128]{2,0,1:T(8,128)S(1)}, f32[128,2,128]{2,0,1:T(8,128)S(1)}, u32[]{:S(2)}, u32[]{:S(2)}) collective-permute-start(f32[128,2,128]{2,0,1:T(8,128)S(1)} %broadcast_multiply_fusion.8), channel_id=1, source_target_pairs={{0,64},{4,68},{8,72},{12,76},{16,80},{20,84},{24,88},{28,92},{32,9... | collective-permute-start | bytes 393224 | tf_op jit(solution)/shard_map/ppermute | solution.py:14
  68.0 1.9 %collective-permute-start.11 = (f32[128,2,128]{2,0,1:T(8,128)S(1)}, f32[128,2,128]{2,0,1:T(8,128)S(1)}, u32[]{:S(2)}, u32[]{:S(2)}) collective-permute-start(f32[128,2,128]{2,0,1:T(8,128)S(1)} %broadcast_multiply_fusion.2), channel_id=1, source_target_pairs={{0,64},{4,68},{8,72},{12,76},{16,80},{20,84},{24,88},{28,92},{32,9... | collective-permute-start | bytes 393224 | tf_op jit(solution)/shard_map/ppermute | solution.py:14
  71.7 2.1 %collective-permute-done.4 = f32[128,2,128]{2,0,1:T(8,128)S(1)} collective-permute-done((f32[128,2,128]{2,0,1:T(8,128)S(1)}, f32[128,2,128]{2,0,1:T(8,128)S(1)}, u32[]{:S(2)}, u32[]{:S(2)}) %collective-permute-start.4) | collective-permute-done | bytes 131104 | tf_op jit(solution)/shard_map/ppermute | solution.py:14
  74.2 9.2 %collective-permute-start.5 = (f32[128,2,128]{2,0,1:T(8,128)S(1)}, f32[128,2,128]{2,0,1:T(8,128)S(1)}, u32[]{:S(2)}, u32[]{:S(2)}) collective-permute-start(f32[128,2,128]{2,0,1:T(8,128)S(1)} %broadcast_multiply_fusion.7), channel_id=1, source_target_pairs={{0,128},{4,132},{8,136},{12,140},{16,144},{20,148},{24,152},{28,15... | collective-permute-start | bytes 393224 | tf_op jit(solution)/shard_map/ppermute | solution.py:14
  83.8 5.4 %collective-permute-start.12 = (f32[128,2,128]{2,0,1:T(8,128)S(1)}, f32[128,2,128]{2,0,1:T(8,128)S(1)}, u32[]{:S(2)}, u32[]{:S(2)}) collective-permute-start(f32[128,2,128]{2,0,1:T(8,128)S(1)} %broadcast_multiply_fusion.1), channel_id=1, source_target_pairs={{0,128},{4,132},{8,136},{12,140},{16,144},{20,148},{24,152},{28,15... | collective-permute-start | bytes 393224 | tf_op jit(solution)/shard_map/ppermute | solution.py:14
  90.4 10.4 %collective-permute-done.5 = f32[128,2,128]{2,0,1:T(8,128)S(1)} collective-permute-done((f32[128,2,128]{2,0,1:T(8,128)S(1)}, f32[128,2,128]{2,0,1:T(8,128)S(1)}, u32[]{:S(2)}, u32[]{:S(2)}) %collective-permute-start.5) | collective-permute-done | bytes 131104 | tf_op jit(solution)/shard_map/ppermute | solution.py:14
  101.2 20.0 %collective-permute-start.6 = (f32[128,2,128]{2,0,1:T(8,128)S(1)}, f32[128,2,128]{2,0,1:T(8,128)S(1)}, u32[]{:S(2)}, u32[]{:S(2)}) collective-permute-start(f32[128,2,128]{2,0,1:T(8,128)S(1)} %broadcast_multiply_fusion.6), channel_id=1, source_target_pairs={{0,256},{4,260},{8,264},{12,268},{16,272},{20,276},{24,280},{28,28... | collective-permute-start | bytes 393224 | tf_op jit(solution)/shard_map/ppermute | solution.py:14
  121.6 2.1 %collective-permute-start.13 = (f32[128,2,128]{2,0,1:T(8,128)S(1)}, f32[128,2,128]{2,0,1:T(8,128)S(1)}, u32[]{:S(2)}, u32[]{:S(2)}) collective-permute-start(f32[128,2,128]{2,0,1:T(8,128)S(1)} %broadcast_multiply_fusion), channel_id=1, source_target_pairs={{0,256},{4,260},{8,264},{12,268},{16,272},{20,276},{24,280},{28,28... | collective-permute-start | bytes 393224 | tf_op jit(solution)/shard_map/ppermute | solution.py:14
  125.3 8.4 %collective-permute-done.6 = f32[128,2,128]{2,0,1:T(8,128)S(1)} collective-permute-done((f32[128,2,128]{2,0,1:T(8,128)S(1)}, f32[128,2,128]{2,0,1:T(8,128)S(1)}, u32[]{:S(2)}, u32[]{:S(2)}) %collective-permute-start.6) | collective-permute-done | bytes 131104 | tf_op jit(solution)/shard_map/ppermute | solution.py:14
  134.2 3.0 %collective-permute-done.13 = f32[128,2,128]{2,0,1:T(8,128)S(1)} collective-permute-done((f32[128,2,128]{2,0,1:T(8,128)S(1)}, f32[128,2,128]{2,0,1:T(8,128)S(1)}, u32[]{:S(2)}, u32[]{:S(2)}) %collective-permute-start.13) | collective-permute-done | bytes 131104 | tf_op jit(solution)/shard_map/ppermute | solution.py:14
  151.3 1.3 fusion.9
  (213 shorter events, 40.6 us)
Async XLA Ops:
  1.6 0.7 copy-start.3
  1.6 2.6 %copy-start.2 = (bf16[512,256]{1,0:T(8,128)(2,1)S(1)}, bf16[512,256]{1,0:T(8,128)(2,1)}, u32[]{:S(2)}) copy-start(bf16[512,256]{1,0:T(8,128)(2,1)} %param.5) | copy-start | bytes 786436
  2.3 24.7 %collective-permute-start = (f32[128,2,128]{2,0,1:T(8,128)}, f32[128,2,128]{2,0,1:T(8,128)}, u32[]{:S(2)}, u32[]{:S(2)}) collective-permute-start(f32[128,2,128]{2,0,1:T(8,128)} %copy_multiply_fusion.2), channel_id=1, source_target_pairs={{0,4},{4,0},{8,12},{12,8},{16,20},{20,16},{24,28},{28,24},{32,36},... | collective-permute-start | bytes 393224 | tf_op jit(solution)/shard_map/ppermute | solution.py:14
  5.0 3.1 %copy-start.1 = (bf16[512,256]{1,0:T(8,128)(2,1)S(1)}, bf16[512,256]{1,0:T(8,128)(2,1)}, u32[]{:S(2)}) copy-start(bf16[512,256]{1,0:T(8,128)(2,1)} %param.4) | copy-start | bytes 786436
  5.6 26.8 %collective-permute-start.7 = (f32[128,2,128]{2,0,1:T(8,128)}, f32[128,2,128]{2,0,1:T(8,128)}, u32[]{:S(2)}, u32[]{:S(2)}) collective-permute-start(f32[128,2,128]{2,0,1:T(8,128)} %copy_multiply_fusion.1), channel_id=1, source_target_pairs={{0,4},{4,0},{8,12},{12,8},{16,20},{20,16},{24,28},{28,24},{32,36},... | collective-permute-start | bytes 393224 | tf_op jit(solution)/shard_map/ppermute | solution.py:14
  8.5 1.0 copy-start
  26.8 0.9 copy-start.4
  29.0 10.7 %collective-permute-start.1 = (f32[128,2,128]{2,0,1:T(8,128)S(1)}, f32[128,2,128]{2,0,1:T(8,128)S(1)}, u32[]{:S(2)}, u32[]{:S(2)}) collective-permute-start(f32[128,2,128]{2,0,1:T(8,128)S(1)} %broadcast_multiply_fusion.11), channel_id=1, source_target_pairs={{0,8},{4,12},{8,0},{12,4},{16,24},{20,28},{24,16},{28,20},{32,40},... | collective-permute-start | bytes 393224 | tf_op jit(solution)/shard_map/ppermute | solution.py:14
  33.8 2.7 %copy-start.6 = (f32[128,2,128]{2,1,0:T(2,128)S(1)}, f32[128,2,128]{2,1,0:T(2,128)}, u32[]{:S(2)}) copy-start(f32[128,2,128]{2,1,0:T(2,128)} %reduce_sum.304) | copy-start | bytes 393220
  33.8 12.5 %collective-permute-start.8 = (f32[128,2,128]{2,0,1:T(8,128)S(1)}, f32[128,2,128]{2,0,1:T(8,128)S(1)}, u32[]{:S(2)}, u32[]{:S(2)}) collective-permute-start(f32[128,2,128]{2,0,1:T(8,128)S(1)} %broadcast_multiply_fusion.5), channel_id=1, source_target_pairs={{0,8},{4,12},{8,0},{12,4},{16,24},{20,28},{24,16},{28,20},{32,40},... | collective-permute-start | bytes 393224 | tf_op jit(solution)/shard_map/ppermute | solution.py:14
  41.1 8.7 %collective-permute-start.2 = (f32[128,2,128]{2,0,1:T(8,128)S(1)}, f32[128,2,128]{2,0,1:T(8,128)S(1)}, u32[]{:S(2)}, u32[]{:S(2)}) collective-permute-start(f32[128,2,128]{2,0,1:T(8,128)S(1)} %broadcast_multiply_fusion.10), channel_id=1, source_target_pairs={{0,16},{4,20},{8,24},{12,28},{16,0},{20,4},{24,8},{28,12},{32,48},... | collective-permute-start | bytes 393224 | tf_op jit(solution)/shard_map/ppermute | solution.py:14
  47.6 8.4 %collective-permute-start.9 = (f32[128,2,128]{2,0,1:T(8,128)S(1)}, f32[128,2,128]{2,0,1:T(8,128)S(1)}, u32[]{:S(2)}, u32[]{:S(2)}) collective-permute-start(f32[128,2,128]{2,0,1:T(8,128)S(1)} %broadcast_multiply_fusion.4), channel_id=1, source_target_pairs={{0,16},{4,20},{8,24},{12,28},{16,0},{20,4},{24,8},{28,12},{32,48},... | collective-permute-start | bytes 393224 | tf_op jit(solution)/shard_map/ppermute | solution.py:14
  50.3 11.8 %collective-permute-start.3 = (f32[128,2,128]{2,0,1:T(8,128)S(1)}, f32[128,2,128]{2,0,1:T(8,128)S(1)}, u32[]{:S(2)}, u32[]{:S(2)}) collective-permute-start(f32[128,2,128]{2,0,1:T(8,128)S(1)} %broadcast_multiply_fusion.9), channel_id=1, source_target_pairs={{0,32},{4,36},{8,40},{12,44},{16,48},{20,52},{24,56},{28,60},{32,0... | collective-permute-start | bytes 393224 | tf_op jit(solution)/shard_map/ppermute | solution.py:14
  56.4 11.3 %collective-permute-start.10 = (f32[128,2,128]{2,0,1:T(8,128)S(1)}, f32[128,2,128]{2,0,1:T(8,128)S(1)}, u32[]{:S(2)}, u32[]{:S(2)}) collective-permute-start(f32[128,2,128]{2,0,1:T(8,128)S(1)} %broadcast_multiply_fusion.3), channel_id=1, source_target_pairs={{0,32},{4,36},{8,40},{12,44},{16,48},{20,52},{24,56},{28,60},{32,0... | collective-permute-start | bytes 393224 | tf_op jit(solution)/shard_map/ppermute | solution.py:14
  62.4 11.4 %collective-permute-start.4 = (f32[128,2,128]{2,0,1:T(8,128)S(1)}, f32[128,2,128]{2,0,1:T(8,128)S(1)}, u32[]{:S(2)}, u32[]{:S(2)}) collective-permute-start(f32[128,2,128]{2,0,1:T(8,128)S(1)} %broadcast_multiply_fusion.8), channel_id=1, source_target_pairs={{0,64},{4,68},{8,72},{12,76},{16,80},{20,84},{24,88},{28,92},{32,9... | collective-permute-start | bytes 393224 | tf_op jit(solution)/shard_map/ppermute | solution.py:14
  68.0 15.4 %collective-permute-start.11 = (f32[128,2,128]{2,0,1:T(8,128)S(1)}, f32[128,2,128]{2,0,1:T(8,128)S(1)}, u32[]{:S(2)}, u32[]{:S(2)}) collective-permute-start(f32[128,2,128]{2,0,1:T(8,128)S(1)} %broadcast_multiply_fusion.2), channel_id=1, source_target_pairs={{0,64},{4,68},{8,72},{12,76},{16,80},{20,84},{24,88},{28,92},{32,9... | collective-permute-start | bytes 393224 | tf_op jit(solution)/shard_map/ppermute | solution.py:14
  74.2 26.5 %collective-permute-start.5 = (f32[128,2,128]{2,0,1:T(8,128)S(1)}, f32[128,2,128]{2,0,1:T(8,128)S(1)}, u32[]{:S(2)}, u32[]{:S(2)}) collective-permute-start(f32[128,2,128]{2,0,1:T(8,128)S(1)} %broadcast_multiply_fusion.7), channel_id=1, source_target_pairs={{0,128},{4,132},{8,136},{12,140},{16,144},{20,148},{24,152},{28,15... | collective-permute-start | bytes 393224 | tf_op jit(solution)/shard_map/ppermute | solution.py:14
  83.8 37.3 %collective-permute-start.12 = (f32[128,2,128]{2,0,1:T(8,128)S(1)}, f32[128,2,128]{2,0,1:T(8,128)S(1)}, u32[]{:S(2)}, u32[]{:S(2)}) collective-permute-start(f32[128,2,128]{2,0,1:T(8,128)S(1)} %broadcast_multiply_fusion.1), channel_id=1, source_target_pairs={{0,128},{4,132},{8,136},{12,140},{16,144},{20,148},{24,152},{28,15... | collective-permute-start | bytes 393224 | tf_op jit(solution)/shard_map/ppermute | solution.py:14
  101.2 32.5 %collective-permute-start.6 = (f32[128,2,128]{2,0,1:T(8,128)S(1)}, f32[128,2,128]{2,0,1:T(8,128)S(1)}, u32[]{:S(2)}, u32[]{:S(2)}) collective-permute-start(f32[128,2,128]{2,0,1:T(8,128)S(1)} %broadcast_multiply_fusion.6), channel_id=1, source_target_pairs={{0,256},{4,260},{8,264},{12,268},{16,272},{20,276},{24,280},{28,28... | collective-permute-start | bytes 393224 | tf_op jit(solution)/shard_map/ppermute | solution.py:14
  121.6 15.6 %collective-permute-start.13 = (f32[128,2,128]{2,0,1:T(8,128)S(1)}, f32[128,2,128]{2,0,1:T(8,128)S(1)}, u32[]{:S(2)}, u32[]{:S(2)}) collective-permute-start(f32[128,2,128]{2,0,1:T(8,128)S(1)} %broadcast_multiply_fusion), channel_id=1, source_target_pairs={{0,256},{4,260},{8,264},{12,268},{16,272},{20,276},{24,280},{28,28... | collective-permute-start | bytes 393224 | tf_op jit(solution)/shard_map/ppermute | solution.py:14
  125.2 8.4 %copy-start.14 = (f32[2,2,128]{2,1,0:T(2,128)S(1)}, f32[2,2,128]{2,1,0:T(2,128)}, u32[]{:S(2)}) copy-start(f32[2,2,128]{2,1,0:T(2,128)} %broadcast_multiply_fusion.12) | copy-start | bytes 6148
  138.2 0.7 copy-start.11
  138.2 0.7 copy-start.10
  140.8 0.7 copy-start.12
  140.8 1.0 copy-start.5
  141.9 0.8 copy-start.8
  142.6 0.7 copy-start.9
  143.5 0.7 copy-start.15
  144.1 0.7 copy-start.13
  150.4 0.8 copy-start.7
where the time goes:
time: 154 us; the launch traced here: 153 us
  starting transfers between devices  69.3 us (45%)
  local copies, waits for them, and re-layouts  30.3 us (20%)
  waiting for transfers between devices  25.7 us (17%)
  other arithmetic  15.9 us (10%)
  matrix products  10 us (6%)
    ppermute x14, starting transfers between devices, partner_2(): return lax.ppermute(value, axis, pairs)  69.3 us
    ppermute x14, waiting for transfers between devices, partner_2(): return lax.ppermute(value, axis, pairs)  25.7 us
    reduce_sum x24, other arithmetic, coarsen(): jnp.mean(field.reshape(rows, factor, field.shape[1], field.shape[2]), axi...  8.29 us
    broadcast_in_dim x27, local copies, waits for them, and re-layouts, expand(): jnp.broadcast_to(field[:, None], (field.shape[0], factor) + field.shape[1:])  7.56 us
    unnamed x37, local copies, waits for them, and re-layouts  5.45 us
    mul x9, local copies, waits for them, and re-layouts, on_device(): numer = numer + weight[..., None] * expand(terms[2], factor)  5.44 us
    dot_general x9, matrix products, pair_terms(): jnp.einsum('bhij,bjhd->bihd', probs, value_blocks, precision=lax.Precisio...  5.36 us
    dot_general x9, matrix products, pair_terms(): jnp.einsum('bihd,bjhd->bhij', query_blocks, key_blocks, precision=lax.Pre...  4.67 us
  transfers between devices with their start and end apart: 14, of which 5 were waited for; matrix products, arithmetic and copies ran while one was open for 24% of the time, Pallas kernels for 0%

commit v1 on v0

v1 whole, which is shorter than its diff:
```python
import jax
import jax.numpy as jnp
import numpy as np
from jax import lax
from jax.experimental import pallas as pl
from jax.experimental.pallas import tpu as pltpu
from jax.sharding import PartitionSpec as P

HEADS = 2
DH = 128
GROUP = 256
TOKENS_HERE = 512
WIDE = HEADS * DH
SCALE = DH ** (-0.5)
MESH = pl.DeviceIdType.MESH
HIGHEST = lax.Precision.HIGHEST

FIRST = {2: 0, 3: 128, 4: 192, 5: 224, 6: 240, 7: 248, 8: 252}
COARSE = 256
SLOT = 32
PACK = 3 * DH


def reverse(value, bits):
    out = 0
    for _ in range(bits):
        out = out * 2 + value % 2
        value //= 2
    return out


def averaging():
    order = np.zeros((GROUP, GROUP), np.float32)
    for row in range(GROUP):
        order[row, reverse(row, 8)] = 1.0
    near = np.zeros((GROUP // 2, GROUP), np.float32)
    for row in range(GROUP // 2):
        first = reverse(row, 7) * 2
        near[row, first : first + 2] = 0.5
    far = np.zeros((COARSE, TOKENS_HERE), np.float32)
    for level in range(2, 9):
        rows = GROUP >> level
        for group in range(2):
            for row in range(rows):
                first = group * GROUP + (reverse(row, 8 - level) << level)
                far[FIRST[level] + group * rows + row, first : first + (1 << level)] = 0.5**level
    tile = np.zeros((48, SLOT), np.float32)
    for row in range(16):
        tile[row, row] = 1.0
        tile[16 + row, 16 + row // 8 * 4 + row % 4] = 1.0
        tile[32 + row, 24 + row // 8 * 2 + row % 2] = 1.0
    return np.concatenate([order, near]), far, tile


def contract_last(a, b, precision=None):
    return lax.dot_general(
        a, b, (((1,), (1,)), ((), ())), precision=precision, preferred_element_type=jnp.float32
    )


def terms(q, k, v, weight):
    scores = contract_last(q, k, HIGHEST) * SCALE
    top = jnp.max(scores, axis=1, keepdims=True)
    probs = jnp.exp(scores - top)
    den = weight * jnp.sum(probs, axis=1, keepdims=True)
    num = weight * jnp.dot(probs, v, precision=HIGHEST, preferred_element_type=jnp.float32)
    return top, den, num


def merge(a, b):
    top = jnp.maximum(a[0], b[0])
    wa = jnp.exp(a[0] - top)
    wb = jnp.exp(b[0] - top)
    return top, wa * a[1] + wb * b[1], wa * a[2] + wb * b[2]


def double(a):
    return tuple(jnp.concatenate([x, x], axis=0) for x in a)


def head_cols(h):
    return slice(h * DH, (h + 1) * DH)


def pack(parts):
    (top0, den0, num0), (top1, den1, num1) = parts
    rows = num0.shape[0]
    lane = lax.broadcasted_iota(jnp.int32, (rows, DH), 1)
    stats = jnp.where(
        lane < 64, jnp.where(lane < 32, top0, den0), jnp.where(lane < 96, top1, den1)
    )
    return jnp.concatenate([num0, num1, stats], axis=1)


def unpack(x, h):
    at = WIDE + 64 * h
    return x[:, at : at + 1], x[:, at + 32 : at + 33], x[:, head_cols(h)]


def combine(slots):
    out = []
    for h in range(HEADS):
        parts = [unpack(x, h) for x in slots]
        while len(parts) > 1:
            parts = [merge(parts[i], parts[i + 1]) for i in range(0, len(parts), 2)]
        out.append(parts[0])
    return out


def level_of(k):
    return 5 + (k.bit_length() - 1)


def kernel(
    q_hbm, k_hbm, v_hbm, near_hbm, far_hbm, tile_hbm, out_ref,
    q, k, v, near, far, tile,
    kvc, qc, kv2, kv3, kv4, kvz, qg, ret, got, ret8, got8, state,
    load, z_send, z_recv, n_send, n_recv, q_send, q_recv, r_send, r_recv, e_send, e_recv,
):
    me = lax.axis_index("ctx")
    head = lax.axis_index("head")
    z = me // 8

    def peer(mask):
        return (jnp.bitwise_xor(me, mask), head)

    def upper(bit):
        return z // (1 << bit) % 2 == 1

    loads = [
        pltpu.make_async_copy(a, b, load.at[i])
        for i, (a, b) in enumerate(
            [(far_hbm, far), (k_hbm, k), (v_hbm, v), (q_hbm, q), (near_hbm, near), (tile_hbm, tile)]
        )
    ]
    for copy in loads:
        copy.start()

    for m in range(1, 8):
        got8[m * 8 : (m + 1) * 8, :] = jnp.zeros((8, PACK), jnp.float32)

    barrier = pltpu.get_barrier_semaphore()
    for m in range(1, 8):
        pl.semaphore_signal(barrier, inc=1, device_id=peer(m), device_id_type=MESH)
    for bit in range(3, -1, -1):

        @pl.when(jnp.logical_not(upper(bit)))
        def _(bit=bit):
            for j in range(1 << bit, 2 << bit):
                pl.semaphore_signal(barrier, inc=1, device_id=peer(8 * j), device_id_type=MESH)

    def column_copy(j):
        level = level_of(j)
        rows = TOKENS_HERE >> level
        at = (level - 5) * 16 + (j - (1 << (level - 5))) * rows
        return pltpu.make_async_remote_copy(
            kvc.at[pl.ds(FIRST[level], rows)], kvz.at[pl.ds(at, rows)],
            z_send.at[j], z_recv.at[j], device_id=peer(8 * j), device_id_type=MESH,
        )

    def near_copy(i, src, dst, mask):
        return pltpu.make_async_remote_copy(
            src, dst, n_send.at[i], n_recv.at[i], device_id=peer(mask), device_id_type=MESH
        )

    near_copies = [
        near_copy(0, kvc.at[pl.ds(FIRST[2], 128)], kv2, 1),
        near_copy(1, kvc.at[pl.ds(FIRST[3], 64)], kv3.at[pl.ds(0, 64)], 2),
        near_copy(2, kvc.at[pl.ds(FIRST[4], 32)], kv4.at[pl.ds(0, 32)], 4),
        near_copy(3, kvc.at[pl.ds(FIRST[4], 32)], kv4.at[pl.ds(32, 32)], 6),
        near_copy(4, kv3.at[pl.ds(0, 64)], kv3.at[pl.ds(64, 64)], 1),
        near_copy(5, kv4.at[pl.ds(0, 64)], kv4.at[pl.ds(64, 64)], 1),
    ]

    def query_copy(m):
        return pltpu.make_async_remote_copy(
            qg.at[pl.ds(0, SLOT)], qg.at[pl.ds(m * SLOT, SLOT)],
            q_send.at[m], q_recv.at[m], device_id=peer(m), device_id_type=MESH,
        )

    def return_copy(m):
        return pltpu.make_async_remote_copy(
            ret.at[pl.ds(m * SLOT, SLOT)], got.at[pl.ds(m * SLOT, SLOT)],
            r_send.at[m], r_recv.at[m], device_id=peer(m), device_id_type=MESH,
        )

    def last_copy(m):
        return pltpu.make_async_remote_copy(
            ret8.at[pl.ds(m * 8 + 4, 2)], got8.at[pl.ds(m * 8 + 4, 2)],
            e_send.at[m], e_recv.at[m], device_id=peer(m), device_id_type=MESH,
        )

    for copy in loads[:3]:
        copy.wait()
    kvc[:, :WIDE] = jnp.dot(far[...], k[...], preferred_element_type=jnp.float32)
    kvc[:, WIDE:] = jnp.dot(far[...], v[...], preferred_element_type=jnp.float32)

    pl.semaphore_wait(barrier, 7 + z)
    for bit in range(3, -1, -1):

        @pl.when(upper(bit))
        def _(bit=bit):
            for j in range(1 << bit, 2 << bit):
                column_copy(j).start()

    for copy in near_copies[:4]:
        copy.start()
    loads[3].wait()
    qc[...] = jnp.dot(far[...], q[...], preferred_element_type=jnp.float32)
    qg[0:SLOT, :] = qc[FIRST[5] : COARSE, :]
    for m in range(1, 8):
        query_copy(m).start()

    loads[4].wait()
    loads[5].wait()
    ones = jnp.ones((GROUP, DH), jnp.bfloat16)
    q_near, k_near, v_near = [], [], []
    for g in range(2):
        rows = slice(g * GROUP, (g + 1) * GROUP)
        pair = near[GROUP:, :]
        q_near.append(jnp.dot(pair, q[rows, :], preferred_element_type=jnp.float32))
        k_near.append(jnp.dot(pair, k[rows, :], preferred_element_type=jnp.float32))
        v_near.append(jnp.dot(pair, v[rows, :], preferred_element_type=jnp.float32))
    level1 = {}
    for g in range(2):
        rows = slice(g * GROUP, (g + 1) * GROUP)
        ordered = jnp.dot(
            near[:GROUP, :], q[rows, :], preferred_element_type=jnp.float32
        ).astype(jnp.bfloat16)
        for h in range(HEADS):
            cols = head_cols(h)
            scores = contract_last(ordered[:, cols], k[rows, cols]) * SCALE
            top = jnp.max(scores, axis=1, keepdims=True)
            probs = jnp.exp(scores - top)
            high = probs.astype(jnp.bfloat16)
            low = (probs - high.astype(jnp.float32)).astype(jnp.bfloat16)
            wide = jnp.concatenate([v[rows, cols], ones], axis=1)
            both = jnp.dot(high, wide, preferred_element_type=jnp.float32) + jnp.dot(
                low, wide, preferred_element_type=jnp.float32
            )
            state[g, h, 0] = jnp.broadcast_to(top, (GROUP, DH))
            state[g, h, 1] = both[:, DH:]
            state[g, h, 2] = both[:, :DH]
            level1[g, h] = terms(
                q_near[g][:, cols], k_near[1 - g][:, cols], v_near[1 - g][:, cols], 2.0
            )

    near_copies[1].wait_recv()
    near_copies[4].start()
    near_copies[2].wait_recv()
    near_copies[3].wait_recv()
    near_copies[5].start()

    near_copies[0].wait_recv()
    level2 = [
        terms(qc[0:128, head_cols(h)], kv2[:, head_cols(h)], kv2[:, head_cols(h + 2)], 4.0)
        for h in range(HEADS)
    ]
    near_copies[4].wait_recv()
    level3 = [
        terms(qc[128:192, head_cols(h)], kv3[:, head_cols(h)], kv3[:, head_cols(h + 2)], 8.0)
        for h in range(HEADS)
    ]
    near_copies[5].wait_recv()
    level4 = [
        terms(qc[192:224, head_cols(h)], kv4[:, head_cols(h)], kv4[:, head_cols(h + 2)], 16.0)
        for h in range(HEADS)
    ]
    for g in range(2):
        for h in range(HEADS):
            joined = tuple(x[g * 16 : (g + 1) * 16] for x in level4[h])
            joined = merge(tuple(x[g * 32 : (g + 1) * 32] for x in level3[h]), double(joined))
            joined = merge(tuple(x[g * 64 : (g + 1) * 64] for x in level2[h]), double(joined))
            joined = double(merge(level1[g, h], double(joined)))
            top, den, num = merge((state[g, h, 0], state[g, h, 1], state[g, h, 2]), joined)
            state[g, h, 0] = top
            state[g, h, 1] = den
            state[g, h, 2] = num

    def take(bit):
        for j in range((2 << bit) - 1, (1 << bit) - 1, -1):
            column_copy(j).wait_recv()

            @pl.when(jnp.logical_not(upper(bit)))
            def _(j=j):
                column_copy(j).start()

    def partial(level, queries):
        at = (level - 5) * 16
        return pack(
            [
                terms(
                    queries[:, head_cols(h)],
                    kvz[at : at + 16, head_cols(h)],
                    kvz[at : at + 16, head_cols(h + 2)],
                    float(2**level),
                )
                for h in range(HEADS)
            ]
        )

    def queries_of(first, rows):
        return jnp.concatenate(
            [qg[m * SLOT + first : m * SLOT + first + rows, :] for m in range(8)], axis=0
        )

    for m in range(1, 8):
        query_copy(m).wait_recv()
    for bit, first, rows in ((0, 0, 16), (1, 16, 8), (2, 24, 8)):
        take(bit)
        result = partial(5 + bit, queries_of(first, rows))
        for m in range(8):
            ret[m * SLOT + first : m * SLOT + first + rows, :] = result[m * rows : (m + 1) * rows]
    for m in range(1, 8):
        return_copy(m).start()
    for m in range(1, 8):
        return_copy(m).wait_recv()
    parts = combine([ret[0:SLOT, :]] + [got[m * SLOT : (m + 1) * SLOT, :] for m in range(1, 8)])
    spread = jnp.dot(tile[...], pack(parts), precision=HIGHEST, preferred_element_type=jnp.float32)
    for g in range(2):
        for h in range(HEADS):
            five, six, seven = (
                unpack(spread[16 * i + 8 * g : 16 * i + 8 * g + 8, :], h) for i in range(3)
            )
            joined = merge(five, merge(six, seven))
            for _ in range(5):
                joined = double(joined)
            top, den, num = merge((state[g, h, 0], state[g, h, 1], state[g, h, 2]), joined)
            state[g, h, 0] = top
            state[g, h, 1] = den
            state[g, h, 2] = num

    queries = queries_of(24, 8)
    take(3)
    ret8[...] = partial(8, queries)
    for m in range(1, 8):
        last_copy(m).start()
    for m in range(1, 8):
        last_copy(m).wait_recv()
    parts = combine([ret8[0:8, :]] + [got8[m * 8 : (m + 1) * 8, :] for m in range(1, 8)])
    for g in range(2):
        attended = []
        for h in range(HEADS):
            row = tuple(x[4 + g : 5 + g, :] for x in parts[h])
            top = jnp.maximum(state[g, h, 0], row[0])
            wa = jnp.exp(state[g, h, 0] - top)
            wb = jnp.exp(row[0] - top)
            den = wa * state[g, h, 1] + wb * row[1]
            num = wa * state[g, h, 2] + wb * row[2]
            attended.append((num / den).astype(jnp.bfloat16))
        out_ref[g * GROUP : (g + 1) * GROUP, :] = jnp.dot(
            near[:GROUP, :], jnp.concatenate(attended, axis=1), preferred_element_type=jnp.float32
        ).astype(jnp.bfloat16)

    for j in range(1, 16):
        column_copy(j).wait_send()
    for copy in near_copies:
        copy.wait_send()
    for m in range(1, 8):
        query_copy(m).wait_send()
        return_copy(m).wait_send()
        last_copy(m).wait_send()


def on_device(queries, keys, values):
    near, far, tile = averaging()
    near = jnp.asarray(near, jnp.bfloat16)
    far = jnp.asarray(far, jnp.bfloat16)
    tile = jnp.asarray(tile, jnp.float32)
    f32, bf16 = jnp.float32, jnp.bfloat16
    whole = (TOKENS_HERE, WIDE)
    dma = pltpu.SemaphoreType.DMA
    return pl.pallas_call(
        kernel,
        out_shape=jax.ShapeDtypeStruct(whole, bf16),
        in_specs=[pl.BlockSpec(memory_space=pl.ANY)] * 6,
        out_specs=pl.BlockSpec(memory_space=pltpu.VMEM),
        scratch_shapes=[
            pltpu.VMEM(whole, bf16),
            pltpu.VMEM(whole, bf16),
            pltpu.VMEM(whole, bf16),
            pltpu.VMEM(near.shape, bf16),
            pltpu.VMEM(far.shape, bf16),
            pltpu.VMEM(tile.shape, f32),
            pltpu.VMEM((COARSE, 2 * WIDE), f32),
            pltpu.VMEM((COARSE, WIDE), f32),
            pltpu.VMEM((128, 2 * WIDE), f32),
            pltpu.VMEM((128, 2 * WIDE), f32),
            pltpu.VMEM((128, 2 * WIDE), f32),
            pltpu.VMEM((64, 2 * WIDE), f32),
            pltpu.VMEM((8 * SLOT, WIDE), f32),
            pltpu.VMEM((8 * SLOT, PACK), f32),
            pltpu.VMEM((8 * SLOT, PACK), f32),
            pltpu.VMEM((64, PACK), f32),
            pltpu.VMEM((64, PACK), f32),
            pltpu.VMEM((2, HEADS, 3, GROUP, DH), f32),
            dma((6,)),
            dma((16,)),
            dma((16,)),
            dma((6,)),
            dma((6,)),
            dma((8,)),
            dma((8,)),
            dma((8,)),
            dma((8,)),
            dma((8,)),
            dma((8,)),
        ],
        compiler_params=pltpu.CompilerParams(
            collective_id=0, has_side_effects=True, vmem_limit_bytes=48 * 2**20
        ),
    )(queries, keys, values, near, far, tile)


def solution(mesh):
    in_specs = (P("ctx", "head"), P("ctx", "head"), P("ctx", "head"))
    return jax.shard_map(
        on_device, mesh=mesh, in_specs=in_specs, out_specs=P("ctx", "head"), check_vma=False
    )
```

time: 154 us -> 50.4 us (0.33)
  the two profiles are of different devices: /device:TPU:6 before, /device:TPU:449 now
where the time goes in v1:
time: 50.4 us; the launch traced here: 50.1 us
  Pallas kernels  43.9 us (87%)
  local copies, waits for them, and re-layouts  6.17 us (12%)
    pallas_call x1, Pallas kernels, on_device(): pl.pallas_call(kernel, out_shape=jax.ShapeDtypeStruct(whole, bf16), in_sp...  43.9 us
    unnamed x13, local copies, waits for them, and re-layouts  6.17 us

profile of v1, /device:TPU:449, one launch (start us, length us, event | category | flops | bytes accessed | tf_op | source)
XLA Modules:
  0.0 50.1 jit_solution(3460016164269245159)
XLA Ops:
  0.0 0.0 copy-start
  0.0 0.9 %copy-done = bf16[512,256]{1,0:T(8,128)(2,1)S(1)} copy-done((bf16[512,256]{1,0:T(8,128)(2,1)S(1)}, bf16[512,256]{1,0:T(8,128)(2,1)}, u32[]{:S(2)}) %copy-start) | copy-done | bytes 262168
  1.0 0.0 copy-start.1
  1.0 0.9 %copy-done.1 = bf16[512,256]{1,0:T(8,128)(2,1)S(1)} copy-done((bf16[512,256]{1,0:T(8,128)(2,1)S(1)}, bf16[512,256]{1,0:T(8,128)(2,1)}, u32[]{:S(2)}) %copy-start.1) | copy-done | bytes 262168
  1.9 0.0 copy-start.2
  1.9 0.9 %copy-done.2 = bf16[512,256]{1,0:T(8,128)(2,1)S(1)} copy-done((bf16[512,256]{1,0:T(8,128)(2,1)S(1)}, bf16[512,256]{1,0:T(8,128)(2,1)}, u32[]{:S(2)}) %copy-start.2) | copy-done | bytes 262168
  2.9 0.0 copy-start.3
  2.9 0.9 %copy-done.3 = bf16[256,512]{1,0:T(8,128)(2,1)S(1)} copy-done((bf16[256,512]{1,0:T(8,128)(2,1)S(1)}, bf16[256,512]{1,0:T(8,128)(2,1)}, u32[]{:S(2)}) %copy-start.3) | copy-done | bytes 262168
  3.8 0.0 copy-start.4
  3.8 0.9 %copy-done.4 = bf16[384,256]{1,0:T(8,128)(2,1)S(1)} copy-done((bf16[384,256]{1,0:T(8,128)(2,1)S(1)}, bf16[384,256]{1,0:T(8,128)(2,1)}, u32[]{:S(2)}) %copy-start.4) | copy-done | bytes 196632
  4.7 0.0 copy-start.5
  4.7 0.7 %copy-done.5 = f32[48,32]{1,0:T(8,128)S(1)} copy-done((f32[48,32]{1,0:T(8,128)S(1)}, f32[48,32]{1,0:T(8,128)}, u32[]{:S(2)}) %copy-start.5) | copy-done | bytes 6168
  5.5 43.9 %shard_map.64 = bf16[512,256]{1,0:T(8,128)(2,1)S(1)} custom-call(bf16[512,256]{1,0:T(8,128)(2,1)S(1)} %copy-done, bf16[512,256]{1,0:T(8,128)(2,1)S(1)} %copy-done.1, bf16[512,256]{1,0:T(8,128)(2,1)S(1)} %copy-done.2, bf16[384,256]{1,0:T(8,128)(2,1)S(1)} %copy-done.4, bf16[256,512]{1,0:T(8,128)(2,1)S(1)} %copy-done.3, f32[48,32]{1,0:T(8,128)S(1)} %copy-done.5), custom_call_target="tpu_custom_call" | custom-call | tf_op jit(solution)/shard_map/pallas_call | solution.py:373
  49.4 0.7 %copy.8 = bf16[512,256]{1,0:T(8,128)(2,1)} copy(bf16[512,256]{1,0:T(8,128)(2,1)S(1)} %shard_map.64) | data formatting | bytes 524288
Async XLA Ops:
  0.0 0.9 %copy-start = (bf16[512,256]{1,0:T(8,128)(2,1)S(1)}, bf16[512,256]{1,0:T(8,128)(2,1)}, u32[]{:S(2)}) copy-start(bf16[512,256]{1,0:T(8,128)(2,1)} %q_hbm.1) | copy-start | bytes 786436
  1.0 0.9 %copy-start.1 = (bf16[512,256]{1,0:T(8,128)(2,1)S(1)}, bf16[512,256]{1,0:T(8,128)(2,1)}, u32[]{:S(2)}) copy-start(bf16[512,256]{1,0:T(8,128)(2,1)} %k_hbm.1) | copy-start | bytes 786436
  1.9 0.9 %copy-start.2 = (bf16[512,256]{1,0:T(8,128)(2,1)S(1)}, bf16[512,256]{1,0:T(8,128)(2,1)}, u32[]{:S(2)}) copy-start(bf16[512,256]{1,0:T(8,128)(2,1)} %v_hbm.1) | copy-start | bytes 786436
  2.9 0.9 %copy-start.3 = (bf16[256,512]{1,0:T(8,128)(2,1)S(1)}, bf16[256,512]{1,0:T(8,128)(2,1)}, u32[]{:S(2)}) copy-start(bf16[256,512]{1,0:T(8,128)(2,1)} %constant.7.clone.far_hbm) | copy-start | bytes 786436
  3.8 0.9 %copy-start.4 = (bf16[384,256]{1,0:T(8,128)(2,1)S(1)}, bf16[384,256]{1,0:T(8,128)(2,1)}, u32[]{:S(2)}) copy-start(bf16[384,256]{1,0:T(8,128)(2,1)} %constant.6.clone.near_hbm) | copy-start | bytes 589828
  4.7 0.7 %copy-start.5 = (f32[48,32]{1,0:T(8,128)S(1)}, f32[48,32]{1,0:T(8,128)}, u32[]{:S(2)}) copy-start(f32[48,32]{1,0:T(8,128)} %constant.8.clone.tile_hbm) | copy-start | bytes 18436

commit v2 on v1

--- a/solution.py
+++ b/solution.py
@@ -114,7 +114,7 @@
 def kernel(
     q_hbm, k_hbm, v_hbm, near_hbm, far_hbm, tile_hbm, out_ref,
     q, k, v, near, far, tile,
-    kvc, qc, kv2, kv3, kv4, kvz, qg, ret, got, ret8, got8, state,
+    kvc, qc, kv2, kv3, kv4, kvz, kvo, qg, q8, ret, got, ret8, got8, state,
     load, z_send, z_recv, n_send, n_recv, q_send, q_recv, r_send, r_recv, e_send, e_recv,
 ):
     me = lax.axis_index("ctx")
@@ -170,17 +170,22 @@
         near_copy(3, kvc.at[pl.ds(FIRST[4], 32)], kv4.at[pl.ds(32, 32)], 6),
         near_copy(4, kv3.at[pl.ds(0, 64)], kv3.at[pl.ds(64, 64)], 1),
         near_copy(5, kv4.at[pl.ds(0, 64)], kv4.at[pl.ds(64, 64)], 1),
+        near_copy(6, kvz.at[pl.ds(0, 48)], kvo, 1),
     ]
 
     def query_copy(m):
+        if m % 2 == 0:
+            src, dst = qg.at[pl.ds(0, SLOT)], qg.at[pl.ds(m // 2 * SLOT, SLOT)]
+        else:
+            src, dst = qg.at[pl.ds(24, 8)], q8.at[pl.ds(m // 2 * 8, 8)]
         return pltpu.make_async_remote_copy(
-            qg.at[pl.ds(0, SLOT)], qg.at[pl.ds(m * SLOT, SLOT)],
-            q_send.at[m], q_recv.at[m], device_id=peer(m), device_id_type=MESH,
+            src, dst, q_send.at[m], q_recv.at[m], device_id=peer(m), device_id_type=MESH
         )
 
     def return_copy(m):
+        rows = pl.ds(m // 2 * SLOT, SLOT)
         return pltpu.make_async_remote_copy(
-            ret.at[pl.ds(m * SLOT, SLOT)], got.at[pl.ds(m * SLOT, SLOT)],
+            ret.at[rows], got.at[rows],
             r_send.at[m], r_recv.at[m], device_id=peer(m), device_id_type=MESH,
         )
 
@@ -245,6 +250,15 @@
                 q_near[g][:, cols], k_near[1 - g][:, cols], v_near[1 - g][:, cols], 2.0
             )
 
+    def answer(bit, here):
+        @pl.when(jnp.logical_and(here, jnp.logical_not(upper(bit))))
+        def _():
+            for j in range((2 << bit) - 1, (1 << bit) - 1, -1):
+                column_copy(j).wait_recv()
+                column_copy(j).start()
+
+    for bit in range(3):
+        answer(bit, z >= 3)
     near_copies[1].wait_recv()
     near_copies[4].start()
     near_copies[2].wait_recv()
@@ -266,6 +280,7 @@
         terms(qc[192:224, head_cols(h)], kv4[:, head_cols(h)], kv4[:, head_cols(h + 2)], 16.0)
         for h in range(HEADS)
     ]
+    answer(3, z >= 3)
     for g in range(2):
         for h in range(HEADS):
             joined = tuple(x[g * 16 : (g + 1) * 16] for x in level4[h])
@@ -277,45 +292,59 @@
             state[g, h, 1] = den
             state[g, h, 2] = num
 
-    def take(bit):
-        for j in range((2 << bit) - 1, (1 << bit) - 1, -1):
-            column_copy(j).wait_recv()
-
-            @pl.when(jnp.logical_not(upper(bit)))
-            def _(j=j):
-                column_copy(j).start()
-
-    def partial(level, queries):
-        at = (level - 5) * 16
+    def collect(bit):
+        @pl.when(upper(bit))
+        def _():
+            for j in range((2 << bit) - 1, (1 << bit) - 1, -1):
+                column_copy(j).wait_recv()
+
+    def partial(level, queries, fields):
         return pack(
             [
                 terms(
                     queries[:, head_cols(h)],
-                    kvz[at : at + 16, head_cols(h)],
-                    kvz[at : at + 16, head_cols(h + 2)],
+                    fields[:, head_cols(h)],
+                    fields[:, head_cols(h + 2)],
                     float(2**level),
                 )
                 for h in range(HEADS)
             ]
         )
 
-    def queries_of(first, rows):
-        return jnp.concatenate(
-            [qg[m * SLOT + first : m * SLOT + first + rows, :] for m in range(8)], axis=0
-        )
-
+    for bit in range(3):
+        answer(bit, z < 3)
+        collect(bit)
+    near_copies[6].start()
     for m in range(1, 8):
         query_copy(m).wait_recv()
+    near_copies[6].wait_recv()
     for bit, first, rows in ((0, 0, 16), (1, 16, 8), (2, 24, 8)):
-        take(bit)
-        result = partial(5 + bit, queries_of(first, rows))
-        for m in range(8):
-            ret[m * SLOT + first : m * SLOT + first + rows, :] = result[m * rows : (m + 1) * rows]
-    for m in range(1, 8):
+        queries = jnp.concatenate(
+            [qg[i * SLOT + first : i * SLOT + first + rows, :] for i in range(4)], axis=0
+        )
+        fields = jnp.concatenate(
+            [kvz[16 * bit : 16 * bit + 16, :], kvo[16 * bit : 16 * bit + 16, :]], axis=0
+        )
+        result = partial(5 + bit, queries, fields)
+        for i in range(4):
+            ret[i * SLOT + first : i * SLOT + first + rows, :] = result[i * rows : (i + 1) * rows]
+    for m in (2, 4, 6):
         return_copy(m).start()
-    for m in range(1, 8):
+    answer(3, z < 3)
+    collect(3)
+    queries = []
+    for m in range(8):
+        queries.append(
+            q8[m // 2 * 8 : m // 2 * 8 + 8, :]
+            if m % 2
+            else qg[m // 2 * SLOT + 24 : (m // 2 + 1) * SLOT, :]
+        )
+    ret8[...] = partial(8, jnp.concatenate(queries, axis=0), kvz[48:64, :])
+    for m in range(1, 8):
+        last_copy(m).start()
+    for m in (2, 4, 6):
         return_copy(m).wait_recv()
-    parts = combine([ret[0:SLOT, :]] + [got[m * SLOT : (m + 1) * SLOT, :] for m in range(1, 8)])
+    parts = combine([ret[0:SLOT, :]] + [got[i * SLOT : (i + 1) * SLOT, :] for i in range(1, 4)])
     spread = jnp.dot(tile[...], pack(parts), precision=HIGHEST, preferred_element_type=jnp.float32)
     for g in range(2):
         for h in range(HEADS):
@@ -329,12 +358,6 @@
             state[g, h, 0] = top
             state[g, h, 1] = den
             state[g, h, 2] = num
-
-    queries = queries_of(24, 8)
-    take(3)
-    ret8[...] = partial(8, queries)
-    for m in range(1, 8):
-        last_copy(m).start()
     for m in range(1, 8):
         last_copy(m).wait_recv()
     parts = combine([ret8[0:8, :]] + [got8[m * 8 : (m + 1) * 8, :] for m in range(1, 8)])
@@ -358,8 +381,9 @@
         copy.wait_send()
     for m in range(1, 8):
         query_copy(m).wait_send()
+        last_copy(m).wait_send()
+    for m in (2, 4, 6):
         return_copy(m).wait_send()
-        last_copy(m).wait_send()
 
 
 def on_device(queries, keys, values):
@@ -388,17 +412,19 @@
             pltpu.VMEM((128, 2 * WIDE), f32),
             pltpu.VMEM((128, 2 * WIDE), f32),
             pltpu.VMEM((64, 2 * WIDE), f32),
-            pltpu.VMEM((8 * SLOT, WIDE), f32),
-            pltpu.VMEM((8 * SLOT, PACK), f32),
-            pltpu.VMEM((8 * SLOT, PACK), f32),
+            pltpu.VMEM((48, 2 * WIDE), f32),
+            pltpu.VMEM((4 * SLOT, WIDE), f32),
+            pltpu.VMEM((32, WIDE), f32),
+            pltpu.VMEM((4 * SLOT, PACK), f32),
+            pltpu.VMEM((4 * SLOT, PACK), f32),
             pltpu.VMEM((64, PACK), f32),
             pltpu.VMEM((64, PACK), f32),
             pltpu.VMEM((2, HEADS, 3, GROUP, DH), f32),
             dma((6,)),
             dma((16,)),
             dma((16,)),
-            dma((6,)),
-            dma((6,)),
+            dma((7,)),
+            dma((7,)),
             dma((8,)),
             dma((8,)),
             dma((8,)),

time: 50.4 us -> 40.4 us (0.80)
  the two profiles are of different devices: /device:TPU:449 before, /device:TPU:129 now
where the time goes in v2:
time: 40.4 us; the launch traced here: 40.1 us
  Pallas kernels  33.9 us (84%)
  local copies, waits for them, and re-layouts  6.17 us (15%)
    pallas_call x1, Pallas kernels, on_device(): pl.pallas_call(kernel, out_shape=jax.ShapeDtypeStruct(whole, bf16), in_sp...  33.9 us
    unnamed x13, local copies, waits for them, and re-layouts  6.17 us

profile of v2, /device:TPU:129, one launch (start us, length us, event | category | flops | bytes accessed | tf_op | source)
XLA Modules:
  0.0 40.1 jit_solution(2127311666192299508)
XLA Ops:
  0.0 0.0 copy-start
  0.0 0.9 %copy-done = bf16[512,256]{1,0:T(8,128)(2,1)S(1)} copy-done((bf16[512,256]{1,0:T(8,128)(2,1)S(1)}, bf16[512,256]{1,0:T(8,128)(2,1)}, u32[]{:S(2)}) %copy-start) | copy-done | bytes 262168
  1.0 0.0 copy-start.1
  1.0 0.9 %copy-done.1 = bf16[512,256]{1,0:T(8,128)(2,1)S(1)} copy-done((bf16[512,256]{1,0:T(8,128)(2,1)S(1)}, bf16[512,256]{1,0:T(8,128)(2,1)}, u32[]{:S(2)}) %copy-start.1) | copy-done | bytes 262168
  1.9 0.0 copy-start.2
  1.9 0.9 %copy-done.2 = bf16[512,256]{1,0:T(8,128)(2,1)S(1)} copy-done((bf16[512,256]{1,0:T(8,128)(2,1)S(1)}, bf16[512,256]{1,0:T(8,128)(2,1)}, u32[]{:S(2)}) %copy-start.2) | copy-done | bytes 262168
  2.9 0.0 copy-start.3
  2.9 0.9 %copy-done.3 = bf16[256,512]{1,0:T(8,128)(2,1)S(1)} copy-done((bf16[256,512]{1,0:T(8,128)(2,1)S(1)}, bf16[256,512]{1,0:T(8,128)(2,1)}, u32[]{:S(2)}) %copy-start.3) | copy-done | bytes 262168
  3.8 0.0 copy-start.4
  3.8 0.9 %copy-done.4 = bf16[384,256]{1,0:T(8,128)(2,1)S(1)} copy-done((bf16[384,256]{1,0:T(8,128)(2,1)S(1)}, bf16[384,256]{1,0:T(8,128)(2,1)}, u32[]{:S(2)}) %copy-start.4) | copy-done | bytes 196632
  4.7 0.0 copy-start.5
  4.7 0.7 %copy-done.5 = f32[48,32]{1,0:T(8,128)S(1)} copy-done((f32[48,32]{1,0:T(8,128)S(1)}, f32[48,32]{1,0:T(8,128)}, u32[]{:S(2)}) %copy-start.5) | copy-done | bytes 6168
  5.5 33.9 %shard_map.64 = bf16[512,256]{1,0:T(8,128)(2,1)S(1)} custom-call(bf16[512,256]{1,0:T(8,128)(2,1)S(1)} %copy-done, bf16[512,256]{1,0:T(8,128)(2,1)S(1)} %copy-done.1, bf16[512,256]{1,0:T(8,128)(2,1)S(1)} %copy-done.2, bf16[384,256]{1,0:T(8,128)(2,1)S(1)} %copy-done.4, bf16[256,512]{1,0:T(8,128)(2,1)S(1)} %copy-done.3, f32[48,32]{1,0:T(8,128)S(1)} %copy-done.5), custom_call_target="tpu_custom_call" | custom-call | tf_op jit(solution)/shard_map/pallas_call | solution.py:397
  39.4 0.7 %copy.8 = bf16[512,256]{1,0:T(8,128)(2,1)} copy(bf16[512,256]{1,0:T(8,128)(2,1)S(1)} %shard_map.64) | data formatting | bytes 524288
Async XLA Ops:
  0.0 0.9 %copy-start = (bf16[512,256]{1,0:T(8,128)(2,1)S(1)}, bf16[512,256]{1,0:T(8,128)(2,1)}, u32[]{:S(2)}) copy-start(bf16[512,256]{1,0:T(8,128)(2,1)} %q_hbm.1) | copy-start | bytes 786436
  1.0 0.9 %copy-start.1 = (bf16[512,256]{1,0:T(8,128)(2,1)S(1)}, bf16[512,256]{1,0:T(8,128)(2,1)}, u32[]{:S(2)}) copy-start(bf16[512,256]{1,0:T(8,128)(2,1)} %k_hbm.1) | copy-start | bytes 786436
  1.9 0.9 %copy-start.2 = (bf16[512,256]{1,0:T(8,128)(2,1)S(1)}, bf16[512,256]{1,0:T(8,128)(2,1)}, u32[]{:S(2)}) copy-start(bf16[512,256]{1,0:T(8,128)(2,1)} %v_hbm.1) | copy-start | bytes 786436
  2.9 0.9 %copy-start.3 = (bf16[256,512]{1,0:T(8,128)(2,1)S(1)}, bf16[256,512]{1,0:T(8,128)(2,1)}, u32[]{:S(2)}) copy-start(bf16[256,512]{1,0:T(8,128)(2,1)} %constant.7.clone.far_hbm) | copy-start | bytes 786436
  3.8 0.9 %copy-start.4 = (bf16[384,256]{1,0:T(8,128)(2,1)S(1)}, bf16[384,256]{1,0:T(8,128)(2,1)}, u32[]{:S(2)}) copy-start(bf16[384,256]{1,0:T(8,128)(2,1)} %constant.6.clone.near_hbm) | copy-start | bytes 589828
  4.7 0.7 %copy-start.5 = (f32[48,32]{1,0:T(8,128)S(1)}, f32[48,32]{1,0:T(8,128)}, u32[]{:S(2)}) copy-start(f32[48,32]{1,0:T(8,128)} %constant.8.clone.tile_hbm) | copy-start | bytes 18436

commit v3 on v2

--- a/solution.py
+++ b/solution.py
@@ -58,13 +58,39 @@
     )
 
 
+def halves(x):
+    high = x.astype(jnp.bfloat16)
+    return high, (x - high.astype(jnp.float32)).astype(jnp.bfloat16)
+
+
 def terms(q, k, v, weight):
-    scores = contract_last(q, k, HIGHEST) * SCALE
+    keys = k.shape[0]
+    q_both = jnp.concatenate(halves(q * SCALE), axis=1)
+    k_high, k_low = halves(k)
+    k_high = jnp.concatenate([k_high, k_high], axis=1)
+    k_low = jnp.concatenate([k_low, k_low], axis=1)
+    v_both = jnp.concatenate(halves(v), axis=1)
+    if keys == DH:
+        scores = contract_last(q_both, jnp.concatenate([k_high, k_low], axis=0))
+        scores = scores[:, :DH] + scores[:, DH:]
+    else:
+        scores = contract_last(q_both, k_high) + contract_last(q_both, k_low)
     top = jnp.max(scores, axis=1, keepdims=True)
     probs = jnp.exp(scores - top)
     den = weight * jnp.sum(probs, axis=1, keepdims=True)
-    num = weight * jnp.dot(probs, v, precision=HIGHEST, preferred_element_type=jnp.float32)
-    return top, den, num
+    p_high, p_low = halves(probs * weight)
+    if keys == DH:
+        p_both = jnp.concatenate([p_high, p_low], axis=1)
+        num = jnp.dot(
+            p_both,
+            jnp.concatenate([v_both, v_both], axis=0),
+            preferred_element_type=jnp.float32,
+        )
+    else:
+        num = jnp.dot(p_high, v_both, preferred_element_type=jnp.float32) + jnp.dot(
+            p_low, v_both, preferred_element_type=jnp.float32
+        )
+    return top, den, num[:, :DH] + num[:, DH:]
 
 
 def merge(a, b):
@@ -258,7 +284,7 @@
                 column_copy(j).start()
 
     for bit in range(3):
-        answer(bit, z >= 3)
+        answer(bit, z >= 0)
     near_copies[1].wait_recv()
     near_copies[4].start()
     near_copies[2].wait_recv()
@@ -280,7 +306,6 @@
         terms(qc[192:224, head_cols(h)], kv4[:, head_cols(h)], kv4[:, head_cols(h + 2)], 16.0)
         for h in range(HEADS)
     ]
-    answer(3, z >= 3)
     for g in range(2):
         for h in range(HEADS):
             joined = tuple(x[g * 16 : (g + 1) * 16] for x in level4[h])
@@ -311,8 +336,8 @@
             ]
         )
 
+    answer(3, z >= 3)
     for bit in range(3):
-        answer(bit, z < 3)
         collect(bit)
     near_copies[6].start()
     for m in range(1, 8):
@@ -433,7 +458,7 @@
             dma((8,)),
         ],
         compiler_params=pltpu.CompilerParams(
-            collective_id=0, has_side_effects=True, vmem_limit_bytes=48 * 2**20
+            collective_id=0, has_side_effects=True, vmem_limit_bytes=54 * 2**20
         ),
     )(queries, keys, values, near, far, tile)
 

time: 40.4 us -> 31.7 us (0.78)
  the two profiles are of different devices: /device:TPU:129 before, /device:TPU:1 now
where the time goes in v3:
time: 31.7 us; the launch traced here: 31.5 us
  Pallas kernels  29.8 us (94%)
  local copies, waits for them, and re-layouts  1.67 us (5%)
    pallas_call x1, Pallas kernels, on_device(): pl.pallas_call(kernel, out_shape=jax.ShapeDtypeStruct(whole, bf16), in_sp...  29.8 us
    unnamed x1, local copies, waits for them, and re-layouts  1.67 us

profile of v3, /device:TPU:1, one launch (start us, length us, event | category | flops | bytes accessed | tf_op | source)
XLA Modules:
  0.0 31.5 jit_solution(16997869384197592880)
XLA Ops:
  0.0 29.8 %shard_map.64 = bf16[512,256]{1,0:T(8,128)(2,1)} custom-call(bf16[512,256]{1,0:T(8,128)(2,1)} %q_hbm.1, bf16[512,256]{1,0:T(8,128)(2,1)} %k_hbm.1, bf16[512,256]{1,0:T(8,128)(2,1)} %v_hbm.1, bf16[384,256]{1,0:T(8,128)(2,1)} %constant.6.clone.near_hbm, bf16[256,512]{1,0:T(8,128)(2,1)} %constant.7.clone.far_hbm, f32[48,32]{1,0:T(8,128)} %constant.8.clone.tile_hbm), custom_call_target="tpu_custom_call" | custom-call | tf_op jit(solution)/shard_map/pallas_call | solution.py:422
  29.8 1.7 %copy.8 = bf16[512,256]{1,0:T(8,128)(2,1)} copy(bf16[512,256]{1,0:T(8,128)(2,1)} %shard_map.64) | data formatting | bytes 524288

commit v4 on v3

--- a/solution.py
+++ b/solution.py
@@ -44,12 +44,17 @@
             for row in range(rows):
                 first = group * GROUP + (reverse(row, 8 - level) << level)
                 far[FIRST[level] + group * rows + row, first : first + (1 << level)] = 0.5**level
-    tile = np.zeros((48, SLOT), np.float32)
-    for row in range(16):
-        tile[row, row] = 1.0
-        tile[16 + row, 16 + row // 8 * 4 + row % 4] = 1.0
-        tile[32 + row, 24 + row // 8 * 2 + row % 2] = 1.0
-    return np.concatenate([order, near]), far, tile
+    return np.concatenate([far, np.concatenate([order, np.pad(near, ((0, 128), (0, 0)))], axis=1)])
+
+
+def spread_rows():
+    row = lax.broadcasted_iota(jnp.int32, (48, SLOT), 0)
+    col = lax.broadcasted_iota(jnp.int32, (48, SLOT), 1)
+    group = row % 16 // 8
+    six = 16 + group * 4 + row % 4
+    seven = 24 + group * 2 + row % 2
+    source = jnp.where(row < 16, row, jnp.where(row < 32, six, seven))
+    return jnp.where(source == col, 1.0, 0.0)
 
 
 def contract_last(a, b, precision=None):
@@ -138,8 +143,8 @@
 
 
 def kernel(
-    q_hbm, k_hbm, v_hbm, near_hbm, far_hbm, tile_hbm, out_ref,
-    q, k, v, near, far, tile,
+    q_hbm, k_hbm, v_hbm, mean_hbm, out_ref,
+    q, k, v, mean,
     kvc, qc, kv2, kv3, kv4, kvz, kvo, qg, q8, ret, got, ret8, got8, state,
     load, z_send, z_recv, n_send, n_recv, q_send, q_recv, r_send, r_recv, e_send, e_recv,
 ):
@@ -150,13 +155,17 @@
     def peer(mask):
         return (jnp.bitwise_xor(me, mask), head)
 
+    def side(bit):
+        own = z // (1 << bit) % 2
+        return (own + z // 8) % 2 if bit == 2 else own
+
     def upper(bit):
-        return z // (1 << bit) % 2 == 1
+        return side(bit) == 1
 
     loads = [
         pltpu.make_async_copy(a, b, load.at[i])
         for i, (a, b) in enumerate(
-            [(far_hbm, far), (k_hbm, k), (v_hbm, v), (q_hbm, q), (near_hbm, near), (tile_hbm, tile)]
+            [(mean_hbm, mean), (k_hbm, k), (v_hbm, v), (q_hbm, q)]
         )
     ]
     for copy in loads:
@@ -223,10 +232,10 @@
 
     for copy in loads[:3]:
         copy.wait()
-    kvc[:, :WIDE] = jnp.dot(far[...], k[...], preferred_element_type=jnp.float32)
-    kvc[:, WIDE:] = jnp.dot(far[...], v[...], preferred_element_type=jnp.float32)
-
-    pl.semaphore_wait(barrier, 7 + z)
+    kvc[:, :WIDE] = jnp.dot(mean[:COARSE, :], k[...], preferred_element_type=jnp.float32)
+    kvc[:, WIDE:] = jnp.dot(mean[:COARSE, :], v[...], preferred_element_type=jnp.float32)
+
+    pl.semaphore_wait(barrier, 7 + sum(side(bit) << bit for bit in range(4)))
     for bit in range(3, -1, -1):
 
         @pl.when(upper(bit))
@@ -237,18 +246,16 @@
     for copy in near_copies[:4]:
         copy.start()
     loads[3].wait()
-    qc[...] = jnp.dot(far[...], q[...], preferred_element_type=jnp.float32)
+    qc[...] = jnp.dot(mean[:COARSE, :], q[...], preferred_element_type=jnp.float32)
     qg[0:SLOT, :] = qc[FIRST[5] : COARSE, :]
     for m in range(1, 8):
         query_copy(m).start()
 
-    loads[4].wait()
-    loads[5].wait()
     ones = jnp.ones((GROUP, DH), jnp.bfloat16)
     q_near, k_near, v_near = [], [], []
     for g in range(2):
         rows = slice(g * GROUP, (g + 1) * GROUP)
-        pair = near[GROUP:, :]
+        pair = mean[COARSE : COARSE + 128, GROUP:]
         q_near.append(jnp.dot(pair, q[rows, :], preferred_element_type=jnp.float32))
         k_near.append(jnp.dot(pair, k[rows, :], preferred_element_type=jnp.float32))
         v_near.append(jnp.dot(pair, v[rows, :], preferred_element_type=jnp.float32))
@@ -256,7 +263,7 @@
     for g in range(2):
         rows = slice(g * GROUP, (g + 1) * GROUP)
         ordered = jnp.dot(
-            near[:GROUP, :], q[rows, :], preferred_element_type=jnp.float32
+            mean[COARSE:, :GROUP], q[rows, :], preferred_element_type=jnp.float32
         ).astype(jnp.bfloat16)
         for h in range(HEADS):
             cols = head_cols(h)
@@ -283,8 +290,9 @@
                 column_copy(j).wait_recv()
                 column_copy(j).start()
 
-    for bit in range(3):
+    for bit in range(2):
         answer(bit, z >= 0)
+    answer(2, z >= 3)
     near_copies[1].wait_recv()
     near_copies[4].start()
     near_copies[2].wait_recv()
@@ -306,6 +314,7 @@
         terms(qc[192:224, head_cols(h)], kv4[:, head_cols(h)], kv4[:, head_cols(h + 2)], 16.0)
         for h in range(HEADS)
     ]
+    answer(2, z < 3)
     for g in range(2):
         for h in range(HEADS):
             joined = tuple(x[g * 16 : (g + 1) * 16] for x in level4[h])
@@ -370,7 +379,7 @@
     for m in (2, 4, 6):
         return_copy(m).wait_recv()
     parts = combine([ret[0:SLOT, :]] + [got[i * SLOT : (i + 1) * SLOT, :] for i in range(1, 4)])
-    spread = jnp.dot(tile[...], pack(parts), precision=HIGHEST, preferred_element_type=jnp.float32)
+    spread = jnp.dot(spread_rows(), pack(parts), precision=HIGHEST, preferred_element_type=jnp.float32)
     for g in range(2):
         for h in range(HEADS):
             five, six, seven = (
@@ -397,7 +406,7 @@
             num = wa * state[g, h, 2] + wb * row[2]
             attended.append((num / den).astype(jnp.bfloat16))
         out_ref[g * GROUP : (g + 1) * GROUP, :] = jnp.dot(
-            near[:GROUP, :], jnp.concatenate(attended, axis=1), preferred_element_type=jnp.float32
+            mean[COARSE:, :GROUP], jnp.concatenate(attended, axis=1), preferred_element_type=jnp.float32
         ).astype(jnp.bfloat16)
 
     for j in range(1, 16):
@@ -412,25 +421,20 @@
 
 
 def on_device(queries, keys, values):
-    near, far, tile = averaging()
-    near = jnp.asarray(near, jnp.bfloat16)
-    far = jnp.asarray(far, jnp.bfloat16)
-    tile = jnp.asarray(tile, jnp.float32)
+    mean = jnp.asarray(averaging(), jnp.bfloat16)
     f32, bf16 = jnp.float32, jnp.bfloat16
     whole = (TOKENS_HERE, WIDE)
     dma = pltpu.SemaphoreType.DMA
     return pl.pallas_call(
         kernel,
         out_shape=jax.ShapeDtypeStruct(whole, bf16),
-        in_specs=[pl.BlockSpec(memory_space=pl.ANY)] * 6,
+        in_specs=[pl.BlockSpec(memory_space=pl.ANY)] * 4,
         out_specs=pl.BlockSpec(memory_space=pltpu.VMEM),
         scratch_shapes=[
             pltpu.VMEM(whole, bf16),
             pltpu.VMEM(whole, bf16),
             pltpu.VMEM(whole, bf16),
-            pltpu.VMEM(near.shape, bf16),
-            pltpu.VMEM(far.shape, bf16),
-            pltpu.VMEM(tile.shape, f32),
+            pltpu.VMEM(mean.shape, bf16),
             pltpu.VMEM((COARSE, 2 * WIDE), f32),
             pltpu.VMEM((COARSE, WIDE), f32),
             pltpu.VMEM((128, 2 * WIDE), f32),
@@ -445,7 +449,7 @@
             pltpu.VMEM((64, PACK), f32),
             pltpu.VMEM((64, PACK), f32),
             pltpu.VMEM((2, HEADS, 3, GROUP, DH), f32),
-            dma((6,)),
+            dma((4,)),
             dma((16,)),
             dma((16,)),
             dma((7,)),
@@ -458,9 +462,9 @@
             dma((8,)),
         ],
         compiler_params=pltpu.CompilerParams(
-            collective_id=0, has_side_effects=True, vmem_limit_bytes=54 * 2**20
+            collective_id=0, has_side_effects=True, vmem_limit_bytes=54900 * 1024
         ),
-    )(queries, keys, values, near, far, tile)
+    )(queries, keys, values, mean)
 
 
 def solution(mesh):

time: 31.7 us -> 28.7 us (0.905)
  Pallas kernels: 29.8 us -> 27.9 us
  local copies, waits for them, and re-layouts: 1.67 us -> 0.71 us
    pallas_call x1, Pallas kernels: 29.8 us -> 27.9 us  [on_device(): pl.pallas_call(kernel, out_shape=jax.ShapeDtypeStruct(whole, bf16), in_sp...]
    unnamed x1, local copies, waits for them, and re-layouts: 1.67 us -> 0.71 us
where the time goes in v4:
time: 28.7 us; the launch traced here: 28.6 us
  Pallas kernels  27.9 us (97%)
  local copies, waits for them, and re-layouts  0.71 us (2%)
    pallas_call x1, Pallas kernels, on_device(): pl.pallas_call(kernel, out_shape=jax.ShapeDtypeStruct(whole, bf16), in_sp...  27.9 us
    unnamed x1, local copies, waits for them, and re-layouts  0.71 us

profile of v4, /device:TPU:1, one launch (start us, length us, event | category | flops | bytes accessed | tf_op | source)
XLA Modules:
  0.0 28.6 jit_solution(9046378613170930406)
XLA Ops:
  0.0 27.9 %shard_map.46 = bf16[512,256]{1,0:T(8,128)(2,1)S(1)} custom-call(bf16[512,256]{1,0:T(8,128)(2,1)} %q_hbm.1, bf16[512,256]{1,0:T(8,128)(2,1)} %k_hbm.1, bf16[512,256]{1,0:T(8,128)(2,1)} %v_hbm.1, bf16[512,512]{1,0:T(8,128)(2,1)} %constant.2.clone.mean_hbm), custom_call_target="tpu_custom_call" | custom-call | tf_op jit(solution)/shard_map/pallas_call | solution.py:428
  27.9 0.7 %copy.6 = bf16[512,256]{1,0:T(8,128)(2,1)} copy(bf16[512,256]{1,0:T(8,128)(2,1)S(1)} %shard_map.46) | data formatting | bytes 524288

commit v5 on v4

--- a/solution.py
+++ b/solution.py
@@ -128,13 +128,27 @@
     return x[:, at : at + 1], x[:, at + 32 : at + 33], x[:, head_cols(h)]
 
 
+def total(items):
+    while len(items) > 1:
+        items = [items[i] + items[i + 1] for i in range(0, len(items), 2)]
+    return items[0]
+
+
 def combine(slots):
     out = []
     for h in range(HEADS):
         parts = [unpack(x, h) for x in slots]
-        while len(parts) > 1:
-            parts = [merge(parts[i], parts[i + 1]) for i in range(0, len(parts), 2)]
-        out.append(parts[0])
+        tops = [p[0] for p in parts]
+        while len(tops) > 1:
+            tops = [jnp.maximum(tops[i], tops[i + 1]) for i in range(0, len(tops), 2)]
+        scaled = [jnp.exp(p[0] - tops[0]) for p in parts]
+        out.append(
+            (
+                tops[0],
+                total([w * p[1] for w, p in zip(scaled, parts)]),
+                total([w * p[2] for w, p in zip(scaled, parts)]),
+            )
+        )
     return out
 
 
@@ -155,20 +169,22 @@
     def peer(mask):
         return (jnp.bitwise_xor(me, mask), head)
 
-    def side(bit):
-        own = z // (1 << bit) % 2
-        return (own + z // 8) % 2 if bit == 2 else own
-
     def upper(bit):
-        return side(bit) == 1
+        return z // (1 << bit) % 2 == 1
 
     loads = [
         pltpu.make_async_copy(a, b, load.at[i])
         for i, (a, b) in enumerate(
-            [(mean_hbm, mean), (k_hbm, k), (v_hbm, v), (q_hbm, q)]
+            [
+                (mean_hbm.at[pl.ds(0, COARSE)], mean.at[pl.ds(0, COARSE)]),
+                (k_hbm, k),
+                (v_hbm, v),
+                (q_hbm, q),
+                (mean_hbm.at[pl.ds(COARSE, COARSE)], mean.at[pl.ds(COARSE, COARSE)]),
+            ]
         )
     ]
-    for copy in loads:
+    for copy in loads[:3]:
         copy.start()
 
     for m in range(1, 8):
@@ -205,7 +221,8 @@
         near_copy(3, kvc.at[pl.ds(FIRST[4], 32)], kv4.at[pl.ds(32, 32)], 6),
         near_copy(4, kv3.at[pl.ds(0, 64)], kv3.at[pl.ds(64, 64)], 1),
         near_copy(5, kv4.at[pl.ds(0, 64)], kv4.at[pl.ds(64, 64)], 1),
-        near_copy(6, kvz.at[pl.ds(0, 48)], kvo, 1),
+        near_copy(6, kvz.at[pl.ds(0, 32)], kvo.at[pl.ds(0, 32)], 1),
+        near_copy(7, kvz.at[pl.ds(32, 16)], kvo.at[pl.ds(32, 16)], 1),
     ]
 
     def query_copy(m):
@@ -218,10 +235,10 @@
         )
 
     def return_copy(m):
-        rows = pl.ds(m // 2 * SLOT, SLOT)
+        rows = pl.ds(m // 2 * SLOT + 24 * (m % 2), 8 if m % 2 else 24)
         return pltpu.make_async_remote_copy(
             ret.at[rows], got.at[rows],
-            r_send.at[m], r_recv.at[m], device_id=peer(m), device_id_type=MESH,
+            r_send.at[m], r_recv.at[m], device_id=peer(m - m % 2), device_id_type=MESH,
         )
 
     def last_copy(m):
@@ -232,10 +249,12 @@
 
     for copy in loads[:3]:
         copy.wait()
+    for copy in loads[3:]:
+        copy.start()
     kvc[:, :WIDE] = jnp.dot(mean[:COARSE, :], k[...], preferred_element_type=jnp.float32)
     kvc[:, WIDE:] = jnp.dot(mean[:COARSE, :], v[...], preferred_element_type=jnp.float32)
 
-    pl.semaphore_wait(barrier, 7 + sum(side(bit) << bit for bit in range(4)))
+    pl.semaphore_wait(barrier, 7 + z)
     for bit in range(3, -1, -1):
 
         @pl.when(upper(bit))
@@ -246,6 +265,7 @@
     for copy in near_copies[:4]:
         copy.start()
     loads[3].wait()
+    loads[4].wait()
     qc[...] = jnp.dot(mean[:COARSE, :], q[...], preferred_element_type=jnp.float32)
     qg[0:SLOT, :] = qc[FIRST[5] : COARSE, :]
     for m in range(1, 8):
@@ -345,14 +365,15 @@
             ]
         )
 
-    answer(3, z >= 3)
-    for bit in range(3):
-        collect(bit)
+    answer(3, z >= 4)
+    collect(0)
+    collect(1)
     near_copies[6].start()
     for m in range(1, 8):
         query_copy(m).wait_recv()
-    near_copies[6].wait_recv()
-    for bit, first, rows in ((0, 0, 16), (1, 16, 8), (2, 24, 8)):
+
+    def return_level(bit):
+        first, rows = ((0, 16), (16, 8), (24, 8))[bit]
         queries = jnp.concatenate(
             [qg[i * SLOT + first : i * SLOT + first + rows, :] for i in range(4)], axis=0
         )
@@ -362,9 +383,19 @@
         result = partial(5 + bit, queries, fields)
         for i in range(4):
             ret[i * SLOT + first : i * SLOT + first + rows, :] = result[i * rows : (i + 1) * rows]
-    for m in (2, 4, 6):
+
+    near_copies[6].wait_recv()
+    return_level(0)
+    return_level(1)
+    for m in (4, 2, 6):
         return_copy(m).start()
-    answer(3, z < 3)
+    collect(2)
+    near_copies[7].start()
+    near_copies[7].wait_recv()
+    return_level(2)
+    for m in (5, 3, 7):
+        return_copy(m).start()
+    answer(3, z < 4)
     collect(3)
     queries = []
     for m in range(8):
@@ -374,9 +405,9 @@
             else qg[m // 2 * SLOT + 24 : (m // 2 + 1) * SLOT, :]
         )
     ret8[...] = partial(8, jnp.concatenate(queries, axis=0), kvz[48:64, :])
-    for m in range(1, 8):
+    for m in (4, 5, 2, 3, 6, 7, 1):
         last_copy(m).start()
-    for m in (2, 4, 6):
+    for m in range(2, 8):
         return_copy(m).wait_recv()
     parts = combine([ret[0:SLOT, :]] + [got[i * SLOT : (i + 1) * SLOT, :] for i in range(1, 4)])
     spread = jnp.dot(spread_rows(), pack(parts), precision=HIGHEST, preferred_element_type=jnp.float32)
@@ -392,32 +423,31 @@
             state[g, h, 0] = top
             state[g, h, 1] = den
             state[g, h, 2] = num
-    for m in range(1, 8):
-        last_copy(m).wait_recv()
-    parts = combine([ret8[0:8, :]] + [got8[m * 8 : (m + 1) * 8, :] for m in range(1, 8)])
-    for g in range(2):
-        attended = []
-        for h in range(HEADS):
-            row = tuple(x[4 + g : 5 + g, :] for x in parts[h])
-            top = jnp.maximum(state[g, h, 0], row[0])
-            wa = jnp.exp(state[g, h, 0] - top)
-            wb = jnp.exp(row[0] - top)
-            den = wa * state[g, h, 1] + wb * row[1]
-            num = wa * state[g, h, 2] + wb * row[2]
-            attended.append((num / den).astype(jnp.bfloat16))
-        out_ref[g * GROUP : (g + 1) * GROUP, :] = jnp.dot(
-            mean[COARSE:, :GROUP], jnp.concatenate(attended, axis=1), preferred_element_type=jnp.float32
-        ).astype(jnp.bfloat16)
-
     for j in range(1, 16):
         column_copy(j).wait_send()
     for copy in near_copies:
         copy.wait_send()
     for m in range(1, 8):
         query_copy(m).wait_send()
-        last_copy(m).wait_send()
-    for m in (2, 4, 6):
+    for m in range(2, 8):
         return_copy(m).wait_send()
+    for m in range(1, 8):
+        last_copy(m).wait()
+    parts = combine([ret8[0:8, :]] + [got8[m * 8 : (m + 1) * 8, :] for m in range(1, 8)])
+    for g in range(2):
+        attended = []
+        for h in range(HEADS):
+            row = tuple(x[4 + g : 5 + g, :] for x in parts[h])
+            gap = row[0] - state[g, h, 0]
+            small = jnp.exp(-jnp.abs(gap))
+            wa = jnp.where(gap > 0.0, small, 1.0)
+            wb = jnp.where(gap > 0.0, 1.0, small)
+            inverse = 1.0 / (wa * state[g, h, 1] + wb * row[1])
+            joined = (wa * inverse) * state[g, h, 2] + (wb * inverse) * row[2]
+            attended.append(joined.astype(jnp.bfloat16))
+        out_ref[g * GROUP : (g + 1) * GROUP, :] = jnp.dot(
+            mean[COARSE:, :GROUP], jnp.concatenate(attended, axis=1), preferred_element_type=jnp.float32
+        ).astype(jnp.bfloat16)
 
 
 def on_device(queries, keys, values):
@@ -449,11 +479,11 @@
             pltpu.VMEM((64, PACK), f32),
             pltpu.VMEM((64, PACK), f32),
             pltpu.VMEM((2, HEADS, 3, GROUP, DH), f32),
-            dma((4,)),
+            dma((5,)),
             dma((16,)),
             dma((16,)),
-            dma((7,)),
-            dma((7,)),
+            dma((8,)),
+            dma((8,)),
             dma((8,)),
             dma((8,)),
             dma((8,)),

time: 28.7 us -> 28.2 us (0.983)
  Pallas kernels: 27.9 us -> 27.1 us
    pallas_call x1, Pallas kernels: 27.9 us -> 27.1 us  [on_device(): pl.pallas_call(kernel, out_shape=jax.ShapeDtypeStruct(whole, bf16), in_sp...]
where the time goes in v5:
time: 28.2 us; the launch traced here: 27.9 us
  Pallas kernels  27.1 us (96%)
  local copies, waits for them, and re-layouts  0.71 us (3%)
    pallas_call x1, Pallas kernels, on_device(): pl.pallas_call(kernel, out_shape=jax.ShapeDtypeStruct(whole, bf16), in_sp...  27.1 us
    unnamed x1, local copies, waits for them, and re-layouts  0.71 us

profile of v5, /device:TPU:1, one launch (start us, length us, event | category | flops | bytes accessed | tf_op | source)
XLA Modules:
  0.0 27.9 jit_solution(4927235689892931230)
XLA Ops:
  0.0 27.1 %shard_map.46 = bf16[512,256]{1,0:T(8,128)(2,1)S(1)} custom-call(bf16[512,256]{1,0:T(8,128)(2,1)} %q_hbm.1, bf16[512,256]{1,0:T(8,128)(2,1)} %k_hbm.1, bf16[512,256]{1,0:T(8,128)(2,1)} %v_hbm.1, bf16[512,512]{1,0:T(8,128)(2,1)} %constant.2.clone.mean_hbm), custom_call_target="tpu_custom_call" | custom-call | tf_op jit(solution)/shard_map/pallas_call | solution.py:458
  27.1 0.7 %copy.6 = bf16[512,256]{1,0:T(8,128)(2,1)} copy(bf16[512,256]{1,0:T(8,128)(2,1)S(1)} %shard_map.46) | data formatting | bytes 524288

commit v6 on v5

--- a/solution.py
+++ b/solution.py
@@ -176,11 +176,12 @@
         pltpu.make_async_copy(a, b, load.at[i])
         for i, (a, b) in enumerate(
             [
-                (mean_hbm.at[pl.ds(0, COARSE)], mean.at[pl.ds(0, COARSE)]),
+                (mean_hbm.at[pl.ds(FIRST[5], SLOT)], mean.at[pl.ds(FIRST[5], SLOT)]),
                 (k_hbm, k),
                 (v_hbm, v),
                 (q_hbm, q),
                 (mean_hbm.at[pl.ds(COARSE, COARSE)], mean.at[pl.ds(COARSE, COARSE)]),
+                (mean_hbm.at[pl.ds(0, FIRST[5])], mean.at[pl.ds(0, FIRST[5])]),
             ]
         )
     ]
@@ -249,10 +250,11 @@
 
     for copy in loads[:3]:
         copy.wait()
-    for copy in loads[3:]:
+    for copy in (loads[5], loads[3], loads[4]):
         copy.start()
-    kvc[:, :WIDE] = jnp.dot(mean[:COARSE, :], k[...], preferred_element_type=jnp.float32)
-    kvc[:, WIDE:] = jnp.dot(mean[:COARSE, :], v[...], preferred_element_type=jnp.float32)
+    far, close = slice(FIRST[5], COARSE), slice(0, FIRST[5])
+    kvc[far, :WIDE] = jnp.dot(mean[far, :], k[...], preferred_element_type=jnp.float32)
+    kvc[far, WIDE:] = jnp.dot(mean[far, :], v[...], preferred_element_type=jnp.float32)
 
     pl.semaphore_wait(barrier, 7 + z)
     for bit in range(3, -1, -1):
@@ -262,6 +264,9 @@
             for j in range(1 << bit, 2 << bit):
                 column_copy(j).start()
 
+    loads[5].wait()
+    kvc[close, :WIDE] = jnp.dot(mean[close, :], k[...], preferred_element_type=jnp.float32)
+    kvc[close, WIDE:] = jnp.dot(mean[close, :], v[...], preferred_element_type=jnp.float32)
     for copy in near_copies[:4]:
         copy.start()
     loads[3].wait()
@@ -479,7 +484,7 @@
             pltpu.VMEM((64, PACK), f32),
             pltpu.VMEM((64, PACK), f32),
             pltpu.VMEM((2, HEADS, 3, GROUP, DH), f32),
-            dma((5,)),
+            dma((6,)),
             dma((16,)),
             dma((16,)),
             dma((8,)),

time: 28.2 us -> 28.2 us (level)
  no operation moved by 1% of the time
where the time goes in v6:
time: 28.2 us; the launch traced here: 28 us
  Pallas kernels  27.3 us (97%)
  local copies, waits for them, and re-layouts  0.71 us (3%)
    pallas_call x1, Pallas kernels, on_device(): pl.pallas_call(kernel, out_shape=jax.ShapeDtypeStruct(whole, bf16), in_sp...  27.3 us
    unnamed x1, local copies, waits for them, and re-layouts  0.71 us

profile of v6, /device:TPU:1, one launch (start us, length us, event | category | flops | bytes accessed | tf_op | source)
XLA Modules:
  0.0 28.0 jit_solution(2155592955963983071)
XLA Ops:
  0.0 27.3 %shard_map.46 = bf16[512,256]{1,0:T(8,128)(2,1)S(1)} custom-call(bf16[512,256]{1,0:T(8,128)(2,1)} %q_hbm.1, bf16[512,256]{1,0:T(8,128)(2,1)} %k_hbm.1, bf16[512,256]{1,0:T(8,128)(2,1)} %v_hbm.1, bf16[512,512]{1,0:T(8,128)(2,1)} %constant.2.clone.mean_hbm), custom_call_target="tpu_custom_call" | custom-call | tf_op jit(solution)/shard_map/pallas_call | solution.py:463
  27.3 0.7 %copy.6 = bf16[512,256]{1,0:T(8,128)(2,1)} copy(bf16[512,256]{1,0:T(8,128)(2,1)S(1)} %shard_map.46) | data formatting | bytes 524288

commit v7 on v6

--- a/solution.py
+++ b/solution.py
@@ -68,9 +68,13 @@
     return high, (x - high.astype(jnp.float32)).astype(jnp.bfloat16)
 
 
+def scaled_halves(q):
+    return jnp.concatenate(halves(q * SCALE), axis=1)
+
+
 def terms(q, k, v, weight):
     keys = k.shape[0]
-    q_both = jnp.concatenate(halves(q * SCALE), axis=1)
+    q_both = q if q.dtype == jnp.bfloat16 else scaled_halves(q)
     k_high, k_low = halves(k)
     k_high = jnp.concatenate([k_high, k_high], axis=1)
     k_low = jnp.concatenate([k_low, k_low], axis=1)
@@ -400,8 +404,6 @@
     return_level(2)
     for m in (5, 3, 7):
         return_copy(m).start()
-    answer(3, z < 4)
-    collect(3)
     queries = []
     for m in range(8):
         queries.append(
@@ -409,7 +411,16 @@
             if m % 2
             else qg[m // 2 * SLOT + 24 : (m // 2 + 1) * SLOT, :]
         )
-    ret8[...] = partial(8, jnp.concatenate(queries, axis=0), kvz[48:64, :])
+    queries = jnp.concatenate(queries, axis=0)
+    last_q = [scaled_halves(queries[:, head_cols(h)]) for h in range(HEADS)]
+    answer(3, z < 4)
+    collect(3)
+    ret8[...] = pack(
+        [
+            terms(last_q[h], kvz[48:64, head_cols(h)], kvz[48:64, head_cols(h + 2)], 256.0)
+            for h in range(HEADS)
+        ]
+    )
     for m in (4, 5, 2, 3, 6, 7, 1):
         last_copy(m).start()
     for m in range(2, 8):

time: 28.2 us -> 28.2 us (level)
  no operation moved by 1% of the time
where the time goes in v7:
time: 28.2 us; the launch traced here: 28 us
  Pallas kernels  27.3 us (97%)
  local copies, waits for them, and re-layouts  0.71 us (3%)
    pallas_call x1, Pallas kernels, on_device(): pl.pallas_call(kernel, out_shape=jax.ShapeDtypeStruct(whole, bf16), in_sp...  27.3 us
    unnamed x1, local copies, waits for them, and re-layouts  0.71 us

profile of v7, /device:TPU:1, one launch (start us, length us, event | category | flops | bytes accessed | tf_op | source)
XLA Modules:
  0.0 28.0 jit_solution(2589910368771920774)
XLA Ops:
  0.0 27.3 %shard_map.46 = bf16[512,256]{1,0:T(8,128)(2,1)S(1)} custom-call(bf16[512,256]{1,0:T(8,128)(2,1)} %q_hbm.1, bf16[512,256]{1,0:T(8,128)(2,1)} %k_hbm.1, bf16[512,256]{1,0:T(8,128)(2,1)} %v_hbm.1, bf16[512,512]{1,0:T(8,128)(2,1)} %constant.2.clone.mean_hbm), custom_call_target="tpu_custom_call" | custom-call | tf_op jit(solution)/shard_map/pallas_call | solution.py:474
  27.3 0.7 %copy.6 = bf16[512,256]{1,0:T(8,128)(2,1)} copy(bf16[512,256]{1,0:T(8,128)(2,1)S(1)} %shard_map.46) | data formatting | bytes 524288
